TPU v7x, 32 devices: a whole 2x2x4 slice. The times are simulated.
32 devices in a mesh: batch: 8 (over y, x, core), mp: 4 (over z).
Axes of the slice: x: 2, y: 2, z: 4, core: 2. Of those that a mesh axis runs over, the one named last changes fastest.
Arguments:
- residual: bfloat16 [8, 64, 8192], P('batch', None, 'mp'), may hold values from -6 to 6
- query_states: bfloat16 [8, 64, 4096], P('batch', None, 'mp')
- key_states: bfloat16 [8, 64, 512], P('batch')
- value_states: bfloat16 [8, 64, 512], P('batch'), may hold values from -6 to 6
- prompt_perm: int32 [8], replicated, may hold values from 0 to 7, each once
- ablated_heads: int32 [8], replicated, may hold values from 0 to 31, as said below
- out_weight: bfloat16 [4096, 8192], P('batch', 'mp'), may hold values from -0.09375 to 0.09375
- rms_gain: float32 [8192], P('mp'), may hold values from 0.1 to 1.9
- gate_weight: bfloat16 [8192, 14336], P('mp', 'batch'), may hold values from -0.0625 to 0.0625
- up_weight: bfloat16 [8192, 14336], P('mp', 'batch'), may hold values from -0.0625 to 0.0625
- down_weight: bfloat16 [14336, 8192], P('batch', 'mp'), may hold values from -0.046875 to 0.046875
Outputs:
- attn_out: bfloat16 [8, 64, 8192], P('batch', None, 'mp')
- mlp_out: bfloat16 [8, 64, 8192], P('batch', None, 'mp')
Inputs may be any that keep to these rules, and one draw needn't show every extreme that they name: `prompt_perm`: each prompt index appears exactly once. `ablated_heads`: 8 different head indices in any order, one of them 32 - 1.
All inputs are finite; a program needn't handle non-finite values.
Results may differ from a plain program's by a relative error of at most 0.035.
Values may be sent and summed in bfloat16 or wider, within the bound.
A program may use at most 128 MiB of HBM per device.

v0:
```python
import functools
import functools
import math

import jax
import jax.numpy as jnp
from jax import lax
from jax.experimental import pallas as pl
from jax.experimental.pallas import tpu as pltpu
from jax.sharding import PartitionSpec as P

D = 8192
HEADS = 32
KV = 4
HD = 128
ABLATED = 8


def heads_kernel(q_ref, k_ref, v_ref, o_ref, blocks, send_line, recv_line, send_owner, recv_owner):
    lines, owners, prompts, length, owned = blocks.shape
    devices = o_ref.shape[0]
    me, m = lax.axis_index("batch"), lax.axis_index("mp")
    barrier = pltpu.get_barrier_semaphore()
    for axis, at, size in (("mp", m, lines), ("batch", me, devices)):
        for k in range(1, size):
            pl.semaphore_signal(
                barrier,
                inc=1,
                device_id={axis: lax.rem(at + k, size)},
                device_id_type=pl.DeviceIdType.MESH,
            )
    rows = lax.broadcasted_iota(jnp.int32, (length, length), 0)
    cols = lax.broadcasted_iota(jnp.int32, (length, length), 1)
    causal = rows >= cols
    heads_here = q_ref.shape[2] // HD

    def line_copy(source, k, j, peer):
        block = blocks.at[source, j]
        return pltpu.make_async_remote_copy(
            src_ref=block,
            dst_ref=block,
            send_sem=send_line.at[k - 1, j],
            recv_sem=recv_line.at[k - 1, j],
            device_id={"mp": peer},
            device_id_type=pl.DeviceIdType.MESH,
        )

    def owner_copy(source, k, j, slot, peer):
        return pltpu.make_async_remote_copy(
            src_ref=blocks.at[source, j],
            dst_ref=o_ref.at[slot],
            send_sem=send_owner.at[k, j],
            recv_sem=recv_owner.at[slot],
            device_id={"batch": peer},
            device_id_type=pl.DeviceIdType.MESH,
        )

    def forward(source, k, j):
        owner = source * owners + j

        @pl.when(owner != me)
        def _():
            owner_copy(source, k, j, me, owner).start()

        @pl.when(owner == me)
        def _():
            o_ref[me] = blocks[source, j]

    for j in range(owners):
        for at in range(0, owned, HD):
            head = j * owned // HD + at // HD
            kv = lax.div(m * heads_here + head, HEADS // KV)
            kv = pl.ds(pl.multiple_of(kv * HD, HD), HD)
            for prompt in range(prompts):
                scores = lax.dot_general(
                    q_ref[prompt, :, head * HD : (head + 1) * HD],
                    k_ref[prompt, :, kv],
                    (((1,), (1,)), ((), ())),
                    preferred_element_type=jnp.float32,
                ) / math.sqrt(HD)
                scores = jnp.where(causal, scores, -1e30)
                highest = jnp.max(scores, axis=-1, keepdims=True)
                weights = jnp.exp(scores - highest)
                probability = weights / jnp.sum(weights, axis=-1, keepdims=True)
                blocks[m, j, prompt, :, at : at + HD] = jnp.dot(
                    probability.astype(jnp.bfloat16),
                    v_ref[prompt, :, kv],
                    preferred_element_type=jnp.float32,
                ).astype(jnp.bfloat16)
        if j == 0:
            pl.semaphore_wait(barrier, lines + devices - 2)
        for k in range(1, lines):
            line_copy(m, k, j, lax.rem(m + k, lines)).start()
        forward(m, 0, j)
    for k in range(1, lines):
        source = lax.rem(m + lines - k, lines)
        for j in range(owners):
            line_copy(source, k, j, source).wait_recv()
            forward(source, k, j)
    for k in range(1, devices):
        other = lax.rem(me + k, devices)
        owner_copy(m, 0, 0, other, other).wait_recv()
    for k in range(lines):
        source = lax.rem(m + lines - k, lines)
        for j in range(owners):
            if k > 0:
                line_copy(m, k, j, source).wait_send()

            @pl.when(source * owners + j != me)
            def _(source=source, k=k, j=j):
                owner_copy(source, k, j, me, source * owners + j).wait_send()


def owned_heads(query_states, key_states, value_states, owned):
    prompts, length, columns = query_states.shape
    devices, lines = lax.axis_size("batch"), lax.axis_size("mp")
    owners = columns // owned
    vmem = pl.BlockSpec(memory_space=pltpu.VMEM)
    dma = pltpu.SemaphoreType.DMA
    return pl.pallas_call(
        heads_kernel,
        in_specs=[vmem] * 3,
        out_specs=vmem,
        out_shape=jax.ShapeDtypeStruct((devices, prompts, length, owned), jnp.bfloat16),
        scratch_shapes=[
            pltpu.VMEM((lines, owners, prompts, length, owned), jnp.bfloat16),
            dma((lines - 1, owners)),
            dma((lines - 1, owners)),
            dma((lines, owners)),
            dma((devices,)),
        ],
        compiler_params=params(4),
    )(query_states, key_states, value_states)


def params(collective_id=None):
    return pltpu.CompilerParams(
        collective_id=collective_id,
        has_side_effects=collective_id is not None,
        vmem_limit_bytes=40 * 2**20,
    )


def swap_kernel(perm_ref, chosen_ref, rows_ref, o_ref):
    chosen = chosen_ref[...] > 0
    for prompt in range(rows_ref.shape[0]):
        own = rows_ref[prompt].astype(jnp.float32)
        other = rows_ref[perm_ref[prompt]].astype(jnp.float32)
        o_ref[prompt] = jnp.where(chosen, other, own).astype(jnp.bfloat16)


def swap(prompt_perm, chosen, rows):
    vmem = pl.BlockSpec(memory_space=pltpu.VMEM)
    return pl.pallas_call(
        swap_kernel,
        in_specs=[pl.BlockSpec(memory_space=pltpu.SMEM), vmem, vmem],
        out_specs=vmem,
        out_shape=jax.ShapeDtypeStruct(rows.shape, rows.dtype),
        compiler_params=params(),
    )(prompt_perm, chosen, rows)


def place(devices):
    me = lax.axis_index("batch")
    core = lax.rem(me, 2)
    return devices // 2, lax.div(me, 2), core, me + 1 - 2 * core


def greet(chips, chip, core, mate):
    barrier = pltpu.get_barrier_semaphore()
    for peer in [mate] + [2 * lax.rem(chip + k, chips) + core for k in range(1, chips)]:
        pl.semaphore_signal(
            barrier, inc=1, device_id={"batch": peer}, device_id_type=pl.DeviceIdType.MESH
        )
    pl.semaphore_wait(barrier, chips)


def send(src, dst, send_sem, recv_sem, peer):
    return pltpu.make_async_remote_copy(
        src_ref=src,
        dst_ref=dst,
        send_sem=send_sem,
        recv_sem=recv_sem,
        device_id={"batch": peer},
        device_id_type=pl.DeviceIdType.MESH,
    )


def scatter_kernel(x_ref, o_ref, near, part, far, send_near, recv_near, send_far, recv_far):
    chips, chip, core, mate = place(x_ref.shape[0])
    greet(chips, chip, core, mate)
    owner = [lax.rem(chip + k, chips) for k in range(chips)]
    order = list(range(1, chips)) + [0]
    to_mate = {}
    for k in order:
        to_mate[k] = send(
            x_ref.at[2 * owner[k] + 1 - core], near.at[k], send_near.at[k], recv_near.at[k], mate
        )
        to_mate[k].start()
    away = []
    for k in range(1, chips):
        to_mate[k].wait_recv()
        target = 2 * owner[k] + core
        part[k - 1] = (x_ref[target].astype(jnp.float32) + near[k].astype(jnp.float32)).astype(
            jnp.bfloat16
        )
        copy = send(
            part.at[k - 1], far.at[k - 1], send_far.at[k - 1], recv_far.at[k - 1], target
        )
        copy.start()
        away.append(copy)
    to_mate[0].wait_recv()
    total = x_ref[2 * chip + core].astype(jnp.float32) + near[0].astype(jnp.float32)
    for k in range(1, chips):
        away[k - 1].wait_recv()
        total = total + far[k - 1].astype(jnp.float32)
    o_ref[...] = total.astype(jnp.bfloat16)
    for k in order:
        to_mate[k].wait_send()
    for copy in away:
        copy.wait_send()


def scatter_sum(x):
    devices, rows, columns = x.shape
    chips = devices // 2
    vmem = pl.BlockSpec(memory_space=pltpu.VMEM)
    return pl.pallas_call(
        scatter_kernel,
        in_specs=[vmem],
        out_specs=vmem,
        out_shape=jax.ShapeDtypeStruct((rows, columns), jnp.bfloat16),
        scratch_shapes=[
            pltpu.VMEM((chips, rows, columns), jnp.bfloat16),
            pltpu.VMEM((chips - 1, rows, columns), jnp.bfloat16),
            pltpu.VMEM((chips - 1, rows, columns), jnp.bfloat16),
            pltpu.SemaphoreType.DMA((chips,)),
            pltpu.SemaphoreType.DMA((chips,)),
            pltpu.SemaphoreType.DMA((chips - 1,)),
            pltpu.SemaphoreType.DMA((chips - 1,)),
        ],
        compiler_params=params(1),
    )(x)


def gather_kernel(devices, x_ref, q_ref, ox_ref, oq_ref, send_far, recv_far, send_near, recv_near):
    chips, chip, core, mate = place(devices)
    me = 2 * chip + core
    greet(chips, chip, core, mate)
    pairs = ((x_ref, ox_ref), (q_ref, oq_ref))
    sent = []
    for k in range(1, chips):
        target = 2 * lax.rem(chip + k, chips) + core
        for i, (src, dst) in enumerate(pairs):
            copy = send(src, dst.at[me], send_far.at[k - 1, i], recv_far.at[k - 1, i], target)
            copy.start()
            sent.append(copy)
    for i, (src, dst) in enumerate(pairs):
        copy = send(src, dst.at[me], send_near.at[0, i], recv_near.at[0, i], mate)
        copy.start()
        sent.append(copy)
    ox_ref[me] = x_ref[...]
    oq_ref[me] = q_ref[...]
    for k in range(1, chips):
        source = 2 * lax.rem(chip + chips - k, chips) + core
        for i, (src, dst) in enumerate(pairs):
            send(
                src, dst.at[source], send_far.at[k - 1, i], recv_far.at[k - 1, i], mate
            ).wait_recv()
            copy = send(
                dst.at[source], dst.at[source], send_near.at[k, i], recv_near.at[k, i], mate
            )
            copy.start()
            sent.append(copy)
    for k in range(chips):
        source = 2 * lax.rem(chip + chips - k, chips) + 1 - core
        for i, (src, dst) in enumerate(pairs):
            send(src, dst.at[source], send_near.at[k, i], recv_near.at[k, i], mate).wait_recv()
    for copy in sent:
        copy.wait_send()


def gather_rows(x, squares):
    devices = lax.axis_size("batch")
    chips = devices // 2
    vmem = pl.BlockSpec(memory_space=pltpu.VMEM)
    return pl.pallas_call(
        functools.partial(gather_kernel, devices),
        in_specs=[vmem, vmem],
        out_specs=[vmem, vmem],
        out_shape=[
            jax.ShapeDtypeStruct((devices, *x.shape), x.dtype),
            jax.ShapeDtypeStruct((devices, *squares.shape), squares.dtype),
        ],
        scratch_shapes=[
            pltpu.SemaphoreType.DMA((chips - 1, 2)),
            pltpu.SemaphoreType.DMA((chips - 1, 2)),
            pltpu.SemaphoreType.DMA((chips, 2)),
            pltpu.SemaphoreType.DMA((chips, 2)),
        ],
        compiler_params=params(2),
    )(x, squares)


def hidden_kernel(
    n, lag, x_ref, sq_ref, gate_ref, up_ref, o_ref, gate_buf, up_buf, own, got, squares,
    weight_sem, send_sum, recv_sum, send_hid, recv_hid, send_sq, recv_sq,
):
    m = lax.axis_index("mp")
    count, _, tokens, w = own.shape
    half = tokens // 2
    rows_of = (pl.ds(half, half), pl.ds(0, half))
    last_of = (n - 1, 0)
    pos_of = (m, n - 1 - m)
    way_of = (1, -1)

    def columns(c):
        return pl.ds(0, w) if count == 1 else pl.ds(pl.multiple_of(c * w, w), w)

    def fetch(c, slot):
        return [
            pltpu.make_async_copy(src.at[:, columns(c)], dst.at[slot], weight_sem.at[slot, i])
            for i, (src, dst) in enumerate(((gate_ref, gate_buf), (up_ref, up_buf)))
        ]

    def remote(src, dst, send_sem, recv_sem, peer):
        return pltpu.make_async_remote_copy(
            src_ref=src,
            dst_ref=dst,
            send_sem=send_sem,
            recv_sem=recv_sem,
            device_id={"mp": peer},
            device_id_type=pl.DeviceIdType.MESH,
        )

    def sum_copy(d, c, peer):
        return remote(
            own.at[c, :, rows_of[d], :],
            got.at[d, c],
            send_sum.at[d, c],
            recv_sum.at[d, c],
            peer,
        )

    def hid_copy(d, c, peer):
        block = o_ref.at[rows_of[d], columns(c)]
        return remote(block, block, send_hid.at[d, c], recv_hid.at[d, c], peer)

    def sq_copy(d, slot):
        return remote(
            sq_ref.at[rows_of[d], :],
            squares.at[slot],
            send_sq.at[d],
            recv_sq.at[slot],
            last_of[d],
        )

    for copy in fetch(0, 0):
        copy.start()
    barrier = pltpu.get_barrier_semaphore()
    for k in range(1, n):
        pl.semaphore_signal(
            barrier,
            inc=1,
            device_id={"mp": lax.rem(m + k, n)},
            device_id_type=pl.DeviceIdType.MESH,
        )
    pl.semaphore_wait(barrier, n - 1)
    for d in range(2):

        @pl.when(m != last_of[d])
        def _(d=d):
            sq_copy(d, m).start()

    def step(t, carry):
        @pl.when(t < count)
        def _():
            slot = lax.rem(t, 2)
            for copy in fetch(t, slot):
                copy.wait()

            @pl.when(t + 1 < count)
            def _():
                for copy in fetch(t + 1, 1 - slot):
                    copy.start()

            x = x_ref[...]
            if w % 128 == 0:
                both = jnp.concatenate([gate_buf[slot], up_buf[slot]], axis=1)
                made = jnp.dot(x, both, preferred_element_type=jnp.float32).astype(jnp.bfloat16)
                own[t, 0] = made[:, :w]
                own[t, 1] = made[:, w:]
            else:
                for i, buf in enumerate((gate_buf, up_buf)):
                    own[t, i] = jnp.dot(
                        x, buf[slot], preferred_element_type=jnp.float32
                    ).astype(jnp.bfloat16)

        for d in range(2):
            pos, rows, way = pos_of[d], rows_of[d], way_of[d]
            c = t - lag * pos
            here = (c >= 0) & (c < count)

            @pl.when(here & (pos == 0))
            def _(d=d, c=c, way=way):
                sum_copy(d, c, m + way).start()

            @pl.when(here & (pos > 0) & (pos < n - 1))
            def _(d=d, c=c, way=way, rows=rows):
                sum_copy(d, c, m - way).wait_recv()
                own[c, :, rows, :] = (
                    own[c, :, rows, :].astype(jnp.float32) + got[d, c].astype(jnp.float32)
                ).astype(jnp.bfloat16)
                sum_copy(d, c, m + way).start()

            @pl.when(here & (pos == n - 1))
            def _(d=d, c=c, way=way, rows=rows):
                @pl.when(c == 0)
                def _():
                    for k in range(1, n):
                        sq_copy(d, n - 1 - k if d == 0 else k).wait_recv()

                total = sq_ref[rows, :]
                for k in range(1, n):
                    total = total + squares[n - 1 - k if d == 0 else k]
                inverse = lax.rsqrt(total / D + 1e-05)[:, :1]
                sum_copy(d, c, m - way).wait_recv()
                summed = own[c, :, rows, :].astype(jnp.float32) + got[d, c].astype(jnp.float32)
                gate = summed[0] * inverse
                up = summed[1] * inverse
                o_ref[rows, columns(c)] = (gate / (1.0 + jnp.exp(-gate)) * up).astype(jnp.bfloat16)
                hid_copy(d, c, m - way).start()

            back = t - lag * (2 * (n - 1) - pos)

            @pl.when((back >= 0) & (back < count) & (pos < n - 1))
            def _(d=d, back=back, way=way, pos=pos):
                hid_copy(d, back, m + way).wait_recv()

                @pl.when(pos > 0)
                def _():
                    hid_copy(d, back, m - way).start()

        return carry

    lax.fori_loop(0, count + 2 * lag * (n - 1), step, 0)

    def finish(c, carry):
        for d in range(2):
            pos, way = pos_of[d], way_of[d]

            @pl.when(pos < n - 1)
            def _(d=d, way=way):
                sum_copy(d, c, m + way).wait_send()

            @pl.when(pos > 0)
            def _(d=d, way=way):
                hid_copy(d, c, m - way).wait_send()

        return carry

    lax.fori_loop(0, count, finish, 0)
    for d in range(2):

        @pl.when(m != last_of[d])
        def _(d=d):
            sq_copy(d, m).wait_send()


def hidden_rows(x, squares, gate_weight, up_weight):
    n = lax.axis_size("mp")
    tokens, depth = x.shape
    width = gate_weight.shape[1]
    w = 128 if width % 128 == 0 else width
    count = width // w
    vmem = pl.BlockSpec(memory_space=pltpu.VMEM)
    anywhere = pl.BlockSpec(memory_space=pl.ANY)
    dma = pltpu.SemaphoreType.DMA
    return pl.pallas_call(
        functools.partial(hidden_kernel, n, 2 if count > 1 else 1),
        in_specs=[vmem, vmem, anywhere, anywhere],
        out_specs=vmem,
        out_shape=jax.ShapeDtypeStruct((tokens, width), jnp.bfloat16),
        scratch_shapes=[
            pltpu.VMEM((2, depth, w), jnp.bfloat16),
            pltpu.VMEM((2, depth, w), jnp.bfloat16),
            pltpu.VMEM((count, 2, tokens, w), jnp.bfloat16),
            pltpu.VMEM((2, count, 2, tokens // 2, w), jnp.bfloat16),
            pltpu.VMEM((n, tokens // 2, 128), jnp.float32),
            dma((2, 2)),
            dma((2, count)),
            dma((2, count)),
            dma((2, count)),
            dma((2, count)),
            dma((2,)),
            dma((n,)),
        ],
        compiler_params=params(3),
    )(x, squares, gate_weight, up_weight)


def body(
    residual,
    query_states,
    key_states,
    value_states,
    prompt_perm,
    ablated_heads,
    out_weight,
    rms_gain,
    gate_weight,
    up_weight,
    down_weight,
):
    prompts_here, length, model_cols = residual.shape
    local_rows = prompts_here * length
    batches = lax.axis_size("batch")
    owned_cols = out_weight.shape[0]
    mine = owned_heads(query_states, key_states, value_states, owned_cols)
    prompts = batches * prompts_here
    mine = mine.reshape(prompts, length, owned_cols)
    head_of_col = (lax.axis_index("batch") * owned_cols + jnp.arange(owned_cols)) // HD
    chosen = jnp.any(head_of_col[:, None] == ablated_heads[None, :], axis=1)
    chosen = jnp.where(chosen, 1.0, 0.0).astype(jnp.float32)[None, :]
    ablated = swap(prompt_perm, chosen, mine).reshape(prompts * length, owned_cols)
    attn_part = jnp.dot(ablated, out_weight, preferred_element_type=jnp.float32)
    attn_out = scatter_sum(attn_part.astype(jnp.bfloat16).reshape(batches, local_rows, model_cols))
    hidden_state = residual.reshape(local_rows, model_cols).astype(jnp.float32) + attn_out.astype(
        jnp.float32
    )
    squares = jnp.sum(hidden_state * hidden_state, axis=1, keepdims=True)
    scaled = (hidden_state * rms_gain[None, :]).astype(jnp.bfloat16)
    block_rows, square_rows = gather_rows(scaled, jnp.broadcast_to(squares, (local_rows, 128)))
    block_rows = block_rows.reshape(batches * local_rows, model_cols)
    square_rows = square_rows.reshape(batches * local_rows, 128)
    hidden = hidden_rows(block_rows, square_rows, gate_weight, up_weight)
    mlp_part = jnp.dot(hidden, down_weight, preferred_element_type=jnp.float32)
    mlp_float = scatter_sum(mlp_part.astype(jnp.bfloat16).reshape(batches, local_rows, model_cols))
    return (
        attn_out.reshape(prompts_here, length, model_cols),
        mlp_float.reshape(prompts_here, length, model_cols),
    )


def solution(mesh):
    placed = (
        P("batch", None, "mp"),
        P("batch", None, "mp"),
        P("batch", None, None),
        P("batch", None, None),
        P(),
        P(),
        P("batch", "mp"),
        P("mp"),
        P("mp", "batch"),
        P("mp", "batch"),
        P("batch", "mp"),
    )
    return jax.shard_map(
        body,
        mesh=mesh,
        in_specs=placed,
        out_specs=(P("batch", None, "mp"), P("batch", None, "mp")),
        check_vma=False,
    )
```

profile of v0, /device:TPU:0, one launch (start us, length us, event | category | flops | bytes accessed | tf_op | source)
XLA Modules:
  0.0 165.9 jit_solution(4397786286263981394)
XLA Ops:
  0.6 0.0 copy-start
  0.7 0.9 compare_reduce_fusion
  1.6 0.0 copy-start.1
  1.6 0.9 copy-done.1
  2.5 0.0 copy-start.2
  2.5 0.8 copy-done.2
  3.3 0.8 copy-done.3
  4.1 20.6 %shard_map.122 = bf16[8,1,64,512]{3,2,1,0:T(8,128)(2,1)S(1)} custom-call(bf16[1,64,1024]{2,1,0:T(8,128)(2,1)S(1)} %copy-done.1, bf16[1,64,512]{2,1,0:T(8,128)(2,1)S(1)} %copy-done.2, bf16[1,64,512]{2,1,0:T(8,128)(2,1)S(1)} %copy-done.3), custom_call_target="tpu_custom_call" | custom-call | tf_op jit(solution)/shard_map/pallas_call | solution.py:120
  24.7 0.0 copy-start.4
  24.7 0.6 copy-done.4
  25.4 0.7 shard_map.123
  26.1 0.0 copy-done
  26.1 0.0 slice-start.1
  26.1 1.3 convolution_convert_fusion.1
  27.3 0.0 copy-start.5
  27.4 0.0 copy-start.6
  27.4 18.4 %shard_map.124 = bf16[64,2048]{1,0:T(8,128)(2,1)S(1)} custom-call(bf16[8,64,2048]{2,1,0:T(8,128)(2,1)S(1)} %bitcast.21), custom_call_target="tpu_custom_call" | custom-call | tf_op jit(solution)/shard_map/pallas_call | solution.py:228
  45.8 0.0 copy-done.5
  45.8 0.0 copy-done.6
  45.8 0.2 multiply_reduce_fusion
  46.0 0.1 broadcast_in_dim.20.q_ref
  46.1 17.4 %shard_map.125 = (bf16[8,64,2048]{2,1,0:T(8,128)(2,1)S(1)}, f32[8,64,128]{2,1,0:T(8,128)S(1)}) custom-call(bf16[64,2048]{1,0:T(8,128)(2,1)S(1)} %get-tuple-element.7.x_ref, f32[64,128]{1,0:T(8,128)S(1)} %broadcast_in_dim.20.q_ref), custom_call_target="tpu_custom_call" | custom-call | tf_op jit(solution)/shard_map/pallas_call | solution.py:287
  63.5 0.0 slice-done
  63.5 0.0 slice-done.1
  63.5 0.0 slice-start.3
  63.5 81.5 %shard_map.126 = bf16[512,1792]{1,0:T(8,128)(2,1)S(1)} custom-call(bf16[512,2048]{1,0:T(8,128)(2,1)S(1)} %bitcast.20, f32[512,128]{1,0:T(8,128)S(1)} %bitcast.26, bf16[2048,1792]{1,0:T(8,128)(2,1)S(1)} %bitcast.18, bf16[2048,1792]{1,0:T(8,128)(2,1)} %up_ref.1), custom_call_target="tpu_custom_call" | custom-call | tf_op jit(solution)/shard_map/pallas_call | solution.py:479
  145.0 0.0 slice-done.2
  145.0 0.0 slice-done.3
  145.0 4.2 %convolution_convert_fusion = bf16[512,2048]{1,0:T(8,128)(2,1)S(1)} fusion(bf16[512,1792]{1,0:T(8,128)(2,1)S(1)} %shard_map.126, bf16[1792,2048]{1,0:T(8,128)(2,1)S(1)} %bitcast.29), kind=kOutput, calls=%fused_computation | convolution fusion | flops 3759144960 | bytes 11272192 | tf_op jit(solution)/shard_map/dot_general | solution.py:537
  149.2 15.4 %shard_map.127 = bf16[64,2048]{1,0:T(8,128)(2,1)S(1)} custom-call(bf16[8,64,2048]{2,1,0:T(8,128)(2,1)S(1)} %bitcast.22), custom_call_target="tpu_custom_call" | custom-call | tf_op jit(solution)/shard_map/pallas_call | solution.py:228
  164.5 0.7 copy.15
  165.2 0.7 copy.16
  (7 shorter events, 0.0 us)
Async XLA Ops:
  0.6 25.4 %copy-start = (bf16[512,2048]{1,0:T(8,128)(2,1)S(1)}, bf16[512,2048]{1,0:T(8,128)(2,1)}, u32[]{:S(2)}) copy-start(bf16[512,2048]{1,0:T(8,128)(2,1)} %param.17) | copy-start | bytes 6291460
  1.6 0.9 copy-start.1
  2.5 0.8 copy-start.2
  3.3 0.8 copy-start.3
  24.7 0.7 copy-start.4
  25.4 38.1 %slice-start = ((s8[7340032]{0:T(1024)(128)(4,1)}), s8[4194304]{0:T(1024)(128)(4,1)S(1)}, s32[]{:S(2)}) async-start(s8[7340032]{0:T(1024)(128)(4,1)} %bitcast.17), calls=%async_computation | async-start | bytes 8388608
  26.1 37.4 %slice-start.1 = ((s8[7340032]{0:T(1024)(128)(4,1)}), s8[3145728]{0:T(1024)(128)(4,1)S(1)}, s32[]{:S(2)}) async-start(s8[7340032]{0:T(1024)(128)(4,1)} %bitcast.17), calls=%async_computation.1 | async-start | bytes 6291456
  27.3 18.4 %copy-start.5 = (bf16[1,64,2048]{2,1,0:T(8,128)(2,1)S(1)}, bf16[1,64,2048]{2,1,0:T(8,128)(2,1)}, u32[]{:S(2)}) copy-start(bf16[1,64,2048]{2,1,0:T(8,128)(2,1)} %param.11) | copy-start | bytes 786436
  27.4 18.4 %copy-start.6 = (f32[2048]{0:T(1024)S(1)}, f32[2048]{0:T(1024)}, u32[]{:S(2)}) copy-start(f32[2048]{0:T(1024)} %param.18) | copy-start | bytes 24580
  46.0 99.0 %slice-start.2 = ((s8[7340032]{0:T(1024)(128)(4,1)}), s8[4194304]{0:T(1024)(128)(4,1)S(1)}, s32[]{:S(2)}) async-start(s8[7340032]{0:T(1024)(128)(4,1)} %bitcast.28), calls=%async_computation.2 | async-start | bytes 8388608
  63.5 81.5 %slice-start.3 = ((s8[7340032]{0:T(1024)(128)(4,1)}), s8[3145728]{0:T(1024)(128)(4,1)S(1)}, s32[]{:S(2)}) async-start(s8[7340032]{0:T(1024)(128)(4,1)} %bitcast.28), calls=%async_computation.3 | async-start | bytes 6291456
where the time goes:
time: 166 us
  Pallas kernels  154 us (93%)
  matrix products  5.42 us (3%)
  local copies, waits for them, and re-layouts  4.75 us (3%)
    pallas_call x1, Pallas kernels, hidden_rows(): pl.pallas_call(functools.partial(hidden_kernel, n, 2 if count > 1 else 1)...  81.5 us
    pallas_call x2, Pallas kernels, scatter_sum(): pl.pallas_call(scatter_kernel, in_specs=[vmem], out_specs=vmem, out_shape...  33.8 us
    pallas_call x1, Pallas kernels, owned_heads(): pl.pallas_call(heads_kernel, in_specs=[vmem] * 3, out_specs=vmem, out_sha...  20.6 us
    pallas_call x1, Pallas kernels, gather_rows(): pl.pallas_call(functools.partial(gather_kernel, devices), in_specs=[vmem,...  17.4 us
    unnamed x24, local copies, waits for them, and re-layouts  4.68 us
    dot_general x1, matrix products, body(): mlp_part = jnp.dot(hidden, down_weight, preferred_element_type=jnp.float32)  4.16 us

commit v1 on v0

v1 whole, which is shorter than its diff:
```python
import functools
import math

import jax
import jax.numpy as jnp
from jax import lax
from jax.experimental import pallas as pl
from jax.experimental.pallas import tpu as pltpu
from jax.sharding import PartitionSpec as P

D = 8192
HEADS = 32
KV = 4
HD = 128
R = 16
LAG = 2
BF16, F32 = jnp.bfloat16, jnp.float32


def remote(src, dst, sems, at, **peer):
    return pltpu.make_async_remote_copy(
        src_ref=src,
        dst_ref=dst,
        send_sem=sems[0].at[at],
        recv_sem=sems[1].at[at],
        device_id=peer,
        device_id_type=pl.DeviceIdType.MESH,
    )


def layer_kernel(
    nb, n, slots,
    perm_ref, ablated_ref, res_hbm, q_hbm, k_hbm, v_hbm, wo_hbm, gain_ref, wg_hbm, wu_hbm, wd_hbm,
    attn_ref, mlp_ref,
    res_buf, q_buf, k_buf, v_buf, wo_buf, wg_buf, wu_buf, wd_buf,
    pmat, line, rows,
    part_a, near_a, mid_a, far_a, part_m, near_m, mid_m, far_m,
    x_all, own_sq, got_sq, inv, own, got, hid,
    small_sem, big_sem, gate_sem, up_sem,
    line_s, line_r, owner_s, owner_r,
    na_s, na_r, fa_s, fa_r, nm_s, nm_r, fm_s, fm_r,
    agf_s, agf_r, agn_s, agn_r, sq_s, sq_r, inv_s, inv_r, sum_s, sum_r, hid_s, hid_r,
):
    b, m = lax.axis_index("batch"), lax.axis_index("mp")
    chips = nb // 2
    core, chip = lax.rem(b, 2), lax.div(b, 2)
    mate = b + 1 - 2 * core
    length, cols_d = res_buf.shape
    chunks = length // R
    _, _, owners, _, owned = line.shape
    pieces, _, w = wg_buf.shape
    half = chips * R
    all_rows = nb * R
    heads_here = q_buf.shape[1] // HD
    ends = (n - 1, 0)
    end = (n - 1) * (1 - core)

    kv = lax.div(m * heads_here, HEADS // KV)
    kv = pl.ds(pl.multiple_of(kv * HD, HD), HD)
    small = [
        pltpu.make_async_copy(src, dst, small_sem.at[i])
        for i, (src, dst) in enumerate(
            (
                (q_hbm.at[0], q_buf),
                (k_hbm.at[0, :, kv], k_buf),
                (v_hbm.at[0, :, kv], v_buf),
                (res_hbm.at[0], res_buf),
            )
        )
    ]
    load_wo = pltpu.make_async_copy(wo_hbm, wo_buf, big_sem.at[0])
    load_wd = pltpu.make_async_copy(wd_hbm, wd_buf, big_sem.at[1])

    def piece(c):
        return pl.ds(0, w) if pieces == 1 else pl.ds(pl.multiple_of(c * w, w), w)

    def load_up(c):
        return (
            pltpu.make_async_copy(wg_hbm.at[:, piece(c)], wg_buf.at[c], gate_sem.at[c]),
            pltpu.make_async_copy(wu_hbm.at[:, piece(c)], wu_buf.at[c], up_sem.at[c]),
        )

    for copy in small:
        copy.start()
    barrier = pltpu.get_barrier_semaphore()
    for axis, at, size in (("mp", m, n), ("batch", b, nb)):
        for k in range(1, size):
            pl.semaphore_signal(
                barrier,
                inc=1,
                device_id={axis: lax.rem(at + k, size)},
                device_id_type=pl.DeviceIdType.MESH,
            )
    load_wo.start()
    for c in range(pieces):
        for copy in load_up(c):
            copy.start()
    load_wd.start()

    at_row = lax.broadcasted_iota(jnp.int32, (R, all_rows), 0)
    at_col = lax.broadcasted_iota(jnp.int32, (R, all_rows), 1)
    for slot in range(nb):
        source = perm_ref[2 * (slot % chips) + slot // chips]
        source = lax.rem(source, 2) * chips + lax.div(source, 2)
        hit = at_col - at_row == source * R
        pmat[slot * R : (slot + 1) * R, :] = jnp.where(hit, 1.0, 0.0).astype(BF16)

    for copy in small[:3]:
        copy.wait()
    q = jnp.concatenate([q_buf[:, h * HD : (h + 1) * HD] for h in range(heads_here)], axis=0)
    scores = lax.dot_general(
        q, k_buf[...], (((1,), (1,)), ((), ())), preferred_element_type=F32
    ) / math.sqrt(HD)
    position = lax.rem(lax.broadcasted_iota(jnp.int32, scores.shape, 0), length)
    causal = position >= lax.broadcasted_iota(jnp.int32, scores.shape, 1)
    scores = jnp.where(causal, scores, -1e30)
    weights = jnp.exp(scores - jnp.max(scores, axis=-1, keepdims=True))
    probability = weights / jnp.sum(weights, axis=-1, keepdims=True)
    mixed = jnp.dot(probability.astype(BF16), v_buf[...], preferred_element_type=F32).astype(BF16)
    for k in range(chunks):
        for h in range(heads_here):
            at = h * HD % owned
            line[m, k, h * HD // owned, :, at : at + HD] = mixed[
                h * length + k * R : h * length + (k + 1) * R
            ]

    def line_copy(source, j, k, peer):
        block = line.at[source, k]
        return remote(block, block, (line_s, line_r), (k, j - 1), mp=peer)

    def owner_copy(source, j, i, k, sender, peer):
        return pltpu.make_async_remote_copy(
            src_ref=line.at[source, k, i],
            dst_ref=rows.at[k, lax.rem(sender, 2), lax.div(sender, 2)],
            send_sem=owner_s.at[k, j, i],
            recv_sem=owner_r.at[k, sender],
            device_id={"batch": peer},
            device_id_type=pl.DeviceIdType.MESH,
        )

    pl.semaphore_wait(barrier, n + nb - 2)
    for k in range(chunks):
        for j in range(1, n):
            line_copy(m, j, k, lax.rem(m + j, n)).start()

    def spread_heads(k):
        for j in range(n):
            source = lax.rem(m + n - j, n)
            if j > 0:
                line_copy(source, j, k, source).wait_recv()
            for i in range(owners):
                owner = source * owners + i

                @pl.when(owner != b)
                def _(source=source, j=j, i=i, owner=owner):
                    owner_copy(source, j, i, k, b, owner).start()

                @pl.when(owner == b)
                def _(source=source, i=i):
                    rows[k, core, chip] = line[source, k, i]

    def near_copy(k, part, near, sems):
        return remote(part.at[k, 1 - core], near.at[k], sems, k, batch=mate)

    def far_copy(k, j, mid, far, sems, peer):
        return remote(mid.at[k, j - 1], far.at[k, j - 1], sems, (k, j - 1), batch=peer)

    scatter_a = (part_a, near_a, mid_a, far_a, (na_s, na_r), (fa_s, fa_r))
    scatter_m = (part_m, near_m, mid_m, far_m, (nm_s, nm_r), (fm_s, fm_r))

    def scatter_far(k, bufs):
        part, near, mid, far, near_sems, far_sems = bufs
        near_copy(k, part, near, near_sems).wait_recv()
        for j in range(1, chips):
            target = lax.rem(chip + j, chips)
            mid[k, j - 1] = (part[k, core, target].astype(F32) + near[k, target].astype(F32)).astype(
                BF16
            )
            far_copy(k, j, mid, far, far_sems, 2 * target + core).start()

    def scatter_total(k, bufs):
        part, near, mid, far, near_sems, far_sems = bufs
        total = part[k, core, chip].astype(F32) + near[k, chip].astype(F32)
        for j in range(1, chips):
            far_copy(k, j, mid, far, far_sems, mate).wait_recv()
            total = total + far[k, j - 1].astype(F32)
        return total

    def multiply_into(k, part, x, weight):
        tile = 512 if cols_d % 512 == 0 else cols_d

        def one(i, carry):
            at = pl.ds(pl.multiple_of(i * tile, tile), tile)
            made = jnp.dot(x, weight[:, at], preferred_element_type=F32).astype(BF16)
            part[k, :, :, :, at] = made.reshape(2, chips, R, tile)
            return carry

        lax.fori_loop(0, cols_d // tile, one, 0)

    def project(k):
        for j in range(1, nb):
            other = lax.rem(b + j, nb)
            owner_copy(m, 0, 0, k, other, other).wait_recv()

        @pl.when(k == 0)
        def _():
            load_wo.wait()

        x = rows[k].reshape(all_rows, owned)
        other = jnp.dot(pmat[...], x, preferred_element_type=F32)
        head = lax.broadcasted_iota(jnp.int32, (all_rows, owned), 1) // HD + b * (owned // HD)
        chosen = head == ablated_ref[0]
        for i in range(1, ablated_ref.shape[0]):
            chosen = chosen | (head == ablated_ref[i])
        x = jnp.where(chosen, other, x.astype(F32)).astype(BF16)
        multiply_into(k, part_a, x, wo_buf)
        near_copy(k, part_a, near_a, (na_s, na_r)).start()

    def rows_at(k):
        return pl.ds(pl.multiple_of(k * R, R), R)

    def gather_far(k, j, source, peer):
        block = x_all.at[k, core, source]
        return remote(block, block, (agf_s, agf_r), (k, j - 1), batch=peer)

    def gather_near(k, j, which, source):
        block = x_all.at[k, which, source]
        return remote(block, block, (agn_s, agn_r), (k, j), batch=mate)

    def square_copy(k, source, peer):
        return pltpu.make_async_remote_copy(
            src_ref=own_sq.at[k],
            dst_ref=got_sq.at[k, source],
            send_sem=sq_s.at[k],
            recv_sem=sq_r.at[k, source],
            device_id={"mp": peer},
            device_id_type=pl.DeviceIdType.MESH,
        )

    def inverse_copy(k, j, source, peer):
        block = inv.at[k, source]
        return pltpu.make_async_remote_copy(
            src_ref=block,
            dst_ref=block,
            send_sem=inv_s.at[k, j - 1],
            recv_sem=inv_r.at[k, source],
            device_id={"batch": peer},
            device_id_type=pl.DeviceIdType.MESH,
        )

    def normalize(k):
        total = scatter_total(k, scatter_a)
        attn_ref[0, rows_at(k), :] = total.astype(BF16)
        state = res_buf[rows_at(k), :].astype(F32) + total
        x_all[k, core, chip] = (state * gain_ref[...].reshape(1, cols_d)).astype(BF16)
        for j in range(1, chips):
            gather_far(k, j, chip, 2 * lax.rem(chip + j, chips) + core).start()
        gather_near(k, 0, core, chip).start()
        squares = jnp.sum(state * state, axis=1, keepdims=True)
        own_sq[k] = jnp.broadcast_to(squares, (R, 128))

        @pl.when(m != end)
        def _():
            square_copy(k, m, end).start()

    def gather_rest(k):
        for j in range(1, chips):
            source = lax.rem(chip + chips - j, chips)
            gather_far(k, j, source, mate).wait_recv()
            gather_near(k, j, core, source).start()

        @pl.when(m == end)
        def _():
            total = own_sq[k]
            for j in range(1, n):
                source = lax.rem(m + j, n)
                square_copy(k, source, source).wait_recv()
                total = total + got_sq[k, source]
            inv[k, chip] = lax.rsqrt(total / D + 1e-05)
            for j in range(1, nb):
                inverse_copy(k, j, chip, lax.rem(b + j, nb)).start()

    pos_of = (m, n - 1 - m)
    way_of = (1, -1)

    def sum_copy(d, u, peer):
        return remote(own.at[u, d], got.at[d, u], (sum_s, sum_r), (d, u), mp=peer)

    def hid_copy(d, k, c, peer):
        block = hid.at[k, d, :, piece(c)]
        return remote(block, block, (hid_s, hid_r), (d, k * pieces + c), mp=peer)

    def unit(t):
        k, c = lax.div(t, slots), lax.rem(t, slots)
        return k, c, (t >= 0) & (t < chunks * slots) & (c < pieces)

    def step(i, carry):
        t = i - slots
        k, c, here = unit(t)

        @pl.when(here)
        def _():
            @pl.when(c == 0)
            def _():
                for j in range(chips):
                    source = lax.rem(chip + chips - j, chips)
                    gather_near(k, j, 1 - core, source).wait_recv()

            @pl.when(k == 0)
            def _():
                for copy in load_up(c):
                    copy.wait()

            x = x_all[k].reshape(all_rows, cols_d)
            for i, weight in enumerate((wg_buf, wu_buf)):
                made = jnp.dot(x, weight[c], preferred_element_type=F32).astype(BF16)
                for d in range(2):
                    own[k * pieces + c, d, i] = made[d * half : (d + 1) * half]

        for d in range(2):
            pos, way = pos_of[d], way_of[d]
            k, c, here = unit(t - LAG * pos)
            u = k * pieces + c

            @pl.when(here & (pos == 0))
            def _(d=d, u=u, way=way):
                sum_copy(d, u, m + way).start()

            @pl.when(here & (pos > 0) & (pos < n - 1))
            def _(d=d, u=u, way=way):
                sum_copy(d, u, m - way).wait_recv()
                own[u, d] = (own[u, d].astype(F32) + got[d, u].astype(F32)).astype(BF16)
                sum_copy(d, u, m + way).start()

            @pl.when(here & (pos == n - 1))
            def _(d=d, k=k, c=c, u=u, way=way):
                @pl.when(c == 0)
                def _():
                    for j in range(chips):
                        source = lax.rem(chip + j, chips)

                        @pl.when((core != d) | (j > 0))
                        def _(source=source):
                            inverse_copy(k, 1, source, mate).wait_recv()

                sum_copy(d, u, m - way).wait_recv()
                inverse = inv[k].reshape(half, 128)[:, :1]
                gate = (own[u, d, 0].astype(F32) + got[d, u, 0].astype(F32)) * inverse
                up = (own[u, d, 1].astype(F32) + got[d, u, 1].astype(F32)) * inverse
                hid[k, d, :, piece(c)] = (gate / (1.0 + jnp.exp(-gate)) * up).astype(BF16)
                hid_copy(d, k, c, m - way).start()

            k, c, here = unit(t - LAG * (2 * (n - 1) - pos))

            @pl.when(here & (pos < n - 1))
            def _(d=d, k=k, c=c, way=way, pos=pos):
                hid_copy(d, k, c, m + way).wait_recv()

                @pl.when(pos > 0)
                def _():
                    hid_copy(d, k, c, m - way).start()

        k, s = lax.div(i, slots), lax.rem(i, slots)
        here = k < chunks
        for at, do in (
            (0, project),
            (1, lambda k: scatter_far(k, scatter_a)),
            (2, normalize),
            (3, gather_rest),
        ):

            @pl.when(here & (s == at))
            def _(do=do, k=k):
                do(k)

        @pl.when((k + 1 < chunks) & (s == 4))
        def _():
            spread_heads(k + 1)

        back = t - LAG * 2 * (n - 1) - (pieces - 1)
        k, s = lax.div(back, slots), lax.rem(back, slots)
        here = (back >= 0) & (k < chunks)

        @pl.when(here & (s == 0))
        def _():
            @pl.when(k == 0)
            def _():
                load_wd.wait()

            multiply_into(k, part_m, hid[k].reshape(all_rows, pieces * w), wd_buf)
            near_copy(k, part_m, near_m, (nm_s, nm_r)).start()

        @pl.when(here & (s == 1))
        def _():
            scatter_far(k, scatter_m)

        @pl.when(here & (s == 2))
        def _():
            mlp_ref[0, rows_at(k), :] = scatter_total(k, scatter_m).astype(BF16)

        return carry

    spread_heads(0)
    small[3].wait()
    last = chunks * slots + pieces - 1 + LAG * 2 * (n - 1) + 3
    lax.fori_loop(0, last, step, 0)

    def finish(k, carry):
        for j in range(1, n):
            line_copy(m, j, k, m).wait_send()
        for j in range(n):
            source = lax.rem(m + n - j, n)
            for i in range(owners):

                @pl.when(source * owners + i != b)
                def _(source=source, j=j, i=i):
                    owner_copy(source, j, i, k, b, mate).wait_send()

        for part, near, mid, far, near_sems, far_sems in (scatter_a, scatter_m):
            near_copy(k, part, near, near_sems).wait_send()
            for j in range(1, chips):
                far_copy(k, j, mid, far, far_sems, mate).wait_send()
        for j in range(1, chips):
            gather_far(k, j, chip, mate).wait_send()
        for j in range(chips):
            gather_near(k, j, core, chip).wait_send()

        @pl.when(m != end)
        def _():
            square_copy(k, m, end).wait_send()

        @pl.when(m == end)
        def _():
            for j in range(1, nb):
                inverse_copy(k, j, chip, mate).wait_send()

        def finish_unit(c, carry):
            for d in range(2):
                pos, way = pos_of[d], way_of[d]

                @pl.when(pos < n - 1)
                def _(d=d, way=way):
                    sum_copy(d, k * pieces + c, m + way).wait_send()

                @pl.when(pos > 0)
                def _(d=d, way=way):
                    hid_copy(d, k, c, m - way).wait_send()

            return carry

        return lax.fori_loop(0, pieces, finish_unit, carry)

    lax.fori_loop(0, chunks, finish, 0)


def body(
    residual, query_states, key_states, value_states, prompt_perm, ablated_heads, out_weight,
    rms_gain, gate_weight, up_weight, down_weight,
):
    _, length, cols_d = residual.shape
    nb, n = lax.axis_size("batch"), lax.axis_size("mp")
    chips = nb // 2
    chunks = length // R
    owned = out_weight.shape[0]
    columns = query_states.shape[2]
    owners = columns // owned
    width = gate_weight.shape[1]
    w = 256 if width % 256 == 0 else width
    pieces = width // w
    slots = max(pieces, 6)
    units = chunks * pieces
    half = chips * R
    vmem = pl.BlockSpec(memory_space=pltpu.VMEM)
    smem = pl.BlockSpec(memory_space=pltpu.SMEM)
    anywhere = pl.BlockSpec(memory_space=pl.ANY)
    dma = pltpu.SemaphoreType.DMA

    def scatter_bufs():
        return [
            pltpu.VMEM((chunks, 2, chips, R, cols_d), BF16),
            pltpu.VMEM((chunks, chips, R, cols_d), BF16),
            pltpu.VMEM((chunks, chips - 1, R, cols_d), BF16),
            pltpu.VMEM((chunks, chips - 1, R, cols_d), BF16),
        ]

    out = jax.ShapeDtypeStruct((1, length, cols_d), BF16)
    return pl.pallas_call(
        functools.partial(layer_kernel, nb, n, slots),
        in_specs=[smem, smem] + [anywhere] * 5 + [vmem] + [anywhere] * 3,
        out_specs=[vmem, vmem],
        out_shape=[out, out],
        scratch_shapes=[
            pltpu.VMEM((length, cols_d), BF16),
            pltpu.VMEM((length, columns), BF16),
            pltpu.VMEM((length, HD), BF16),
            pltpu.VMEM((length, HD), BF16),
            pltpu.VMEM((owned, cols_d), BF16),
            pltpu.VMEM((pieces, cols_d, w), BF16),
            pltpu.VMEM((pieces, cols_d, w), BF16),
            pltpu.VMEM((width, cols_d), BF16),
            pltpu.VMEM((nb * R, nb * R), BF16),
            pltpu.VMEM((n, chunks, owners, R, owned), BF16),
            pltpu.VMEM((chunks, 2, chips, R, owned), BF16),
            *scatter_bufs(),
            *scatter_bufs(),
            pltpu.VMEM((chunks, 2, chips, R, cols_d), BF16),
            pltpu.VMEM((chunks, R, 128), F32),
            pltpu.VMEM((chunks, n, R, 128), F32),
            pltpu.VMEM((chunks, chips, R, 128), F32),
            pltpu.VMEM((units, 2, 2, half, w), BF16),
            pltpu.VMEM((2, units, 2, half, w), BF16),
            pltpu.VMEM((chunks, 2, half, width), BF16),
            dma((4,)),
            dma((2,)),
            dma((pieces,)),
            dma((pieces,)),
            *[dma((chunks, n - 1))] * 2,
            dma((chunks, n, owners)),
            dma((chunks, nb)),
            *[dma((chunks,)), dma((chunks,)), dma((chunks, chips - 1)), dma((chunks, chips - 1))] * 2,
            *[dma((chunks, chips - 1))] * 2,
            *[dma((chunks, chips))] * 2,
            dma((chunks,)),
            dma((chunks, n)),
            dma((chunks, nb - 1)),
            dma((chunks, chips)),
            *[dma((2, units))] * 4,
        ],
        compiler_params=pltpu.CompilerParams(
            collective_id=1, has_side_effects=True, vmem_limit_bytes=60 * 2**20
        ),
    )(
        prompt_perm, ablated_heads, residual, query_states, key_states, value_states, out_weight,
        rms_gain, gate_weight, up_weight, down_weight,
    )


def solution(mesh):
    placed = (
        P("batch", None, "mp"),
        P("batch", None, "mp"),
        P("batch", None, None),
        P("batch", None, None),
        P(),
        P(),
        P("batch", "mp"),
        P("mp"),
        P("mp", "batch"),
        P("mp", "batch"),
        P("batch", "mp"),
    )
    return jax.shard_map(
        body,
        mesh=mesh,
        in_specs=placed,
        out_specs=(P("batch", None, "mp"), P("batch", None, "mp")),
        check_vma=False,
    )
```

time: 166 us -> 147 us (0.89)
  Pallas kernels: 154 us -> 142 us
  matrix products: 5.42 us -> 0 us
    pallas_call x6 -> x1, Pallas kernels: 154 us -> 142 us  [body(): pl.pallas_call(functools.partial(layer_kernel, nb, n, slots), in_specs=[s...]
    dot_general x2 -> x0, matrix products: 5.42 us -> none  [the longest x1 4.16 us: body(): mlp_part = jnp.dot(hidden, down_weight, preferred_element_type=jnp.float32)]
    unnamed x24 -> x2, local copies, waits for them, and re-layouts: 4.68 us -> 3.34 us
where the time goes in v1:
time: 147 us; the launch traced here: 146 us
  Pallas kernels  142 us (97%)
  local copies, waits for them, and re-layouts  3.34 us (2%)
    pallas_call x1, Pallas kernels, body(): pl.pallas_call(functools.partial(layer_kernel, nb, n, slots), in_specs=[s...  142 us
    unnamed x2, local copies, waits for them, and re-layouts  3.34 us

profile of v1, /device:TPU:0, one launch (start us, length us, event | category | flops | bytes accessed | tf_op | source)
XLA Modules:
  0.0 146.4 jit_solution(2493966105632460637)
XLA Ops:
  0.6 142.4 %shard_map.122 = (bf16[1,64,2048]{2,1,0:T(8,128)(2,1)}, bf16[1,64,2048]{2,1,0:T(8,128)(2,1)}) custom-call(s32[8]{0:T(128)} %perm_ref.1, s32[8]{0:T(128)} %ablated_ref.1, bf16[1,64,2048]{2,1,0:T(8,128)(2,1)} %res_hbm.1, bf16[1,64,1024]{2,1,0:T(8,128)(2,1)} %q_hbm.1, bf16[1,64,512]{2,1,0:T(8,128)(2,1)} %k_hbm.1, bf16[1,64,512]{2,1,0:T(8,128)(2,1)} %v_hbm.1, ...), custom_call_target="tpu_custom_call" | custom-call | tf_op jit(solution)/shard_map/pallas_call | solution.py:487
  143.1 1.7 %copy.15 = bf16[1,64,2048]{2,1,0:T(8,128)(2,1)} copy(bf16[1,64,2048]{2,1,0:T(8,128)(2,1)} %get-tuple-element.4) | data formatting | bytes 524288
  144.7 1.7 %copy.16 = bf16[1,64,2048]{2,1,0:T(8,128)(2,1)} copy(bf16[1,64,2048]{2,1,0:T(8,128)(2,1)} %get-tuple-element.5) | data formatting | bytes 524288

commit v2 on v1

v2 whole, which is shorter than its diff:
```python
import functools
import math

import jax
import jax.numpy as jnp
from jax import lax
from jax.experimental import pallas as pl
from jax.experimental.pallas import tpu as pltpu
from jax.sharding import PartitionSpec as P

D = 8192
HEADS = 32
KV = 4
HD = 128
R = 16
LAG = 3
LEAD = 20
VMEM = 60 * 2**20
BF16, F32 = jnp.bfloat16, jnp.float32


def remote(src, dst, send_sem, recv_sem, **peer):
    return pltpu.make_async_remote_copy(
        src_ref=src,
        dst_ref=dst,
        send_sem=send_sem,
        recv_sem=recv_sem,
        device_id=peer,
        device_id_type=pl.DeviceIdType.MESH,
    )


def layer_kernel(
    nb, n, slots, w, joined,
    perm_ref, ablated_ref, res_hbm, q_hbm, k_hbm, v_hbm, wo_hbm, gain_ref, wg_hbm, wu_hbm, wd_hbm,
    attn_ref, mlp_ref,
    res_buf, q_buf, k_buf, v_buf, wo_buf, w_buf, wd_buf,
    pmat, line, rows,
    part_a, near_a, mid_a, far_a, part_m, near_m, mid_m, far_m,
    x_all, own_sq, got_sq, inv, own, got, hid,
    small_sem, big_sem,
    line_s, line_r, owner_s, owner_r,
    na_s, na_r, fa_s, fa_r, nm_s, nm_r, fm_s, fm_r,
    agf_s, agf_r, agn_s, agn_r, sq_s, sq_r, inv_s, inv_r, sum_s, sum_r, hid_s, hid_r,
):
    b, m = lax.axis_index("batch"), lax.axis_index("mp")
    chips = nb // 2
    core, chip = lax.rem(b, 2), lax.div(b, 2)
    mate = b + 1 - 2 * core
    my_slot = core * chips + chip
    length, cols_d = res_buf.shape
    chunks = length // R
    _, _, owners, _, owned = line.shape
    pieces = w_buf.shape[0]
    reuse = sum_r.shape[1]
    half = chips * R
    all_rows = nb * R
    heads_here = q_buf.shape[1] // HD
    end = (n - 1) * (1 - core)

    def slot_of(device):
        return lax.rem(device, 2) * chips + lax.div(device, 2)

    kv = lax.div(m * heads_here, HEADS // KV)
    kv = pl.ds(pl.multiple_of(kv * HD, HD), HD)
    small = [
        pltpu.make_async_copy(src, dst, small_sem.at[i])
        for i, (src, dst) in enumerate(
            (
                (q_hbm.at[0], q_buf),
                (k_hbm.at[0, :, kv], k_buf),
                (v_hbm.at[0, :, kv], v_buf),
                (res_hbm.at[0], res_buf),
            )
        )
    ]
    load_wo = pltpu.make_async_copy(wo_hbm, wo_buf, big_sem.at[0])
    load_wd = pltpu.make_async_copy(wd_hbm, wd_buf, big_sem.at[1])

    def piece(c):
        return pl.ds(0, w) if pieces == 1 else pl.ds(pl.multiple_of(c * w, w), w)

    for copy in small:
        copy.start()
    barrier = pltpu.get_barrier_semaphore()
    for axis, at, size in (("mp", m, n), ("batch", b, nb)):
        for k in range(1, size):
            pl.semaphore_signal(
                barrier,
                inc=1,
                device_id={axis: lax.rem(at + k, size)},
                device_id_type=pl.DeviceIdType.MESH,
            )
    load_wo.start()
    for c in range(pieces):
        for i, src in enumerate((wg_hbm, wu_hbm)):
            dst = w_buf.at[c, :, pl.ds(i * w, w)] if joined else w_buf.at[c, i]
            pltpu.make_async_copy(src.at[:, piece(c)], dst, big_sem.at[2]).start()
    load_wd.start()

    at_row = lax.broadcasted_iota(jnp.int32, (R, all_rows), 0)
    at_col = lax.broadcasted_iota(jnp.int32, (R, all_rows), 1)
    for slot in range(nb):
        source = slot_of(perm_ref[2 * (slot % chips) + slot // chips])
        hit = at_col - at_row == source * R
        pmat[slot * R : (slot + 1) * R, :] = jnp.where(hit, 1.0, 0.0).astype(BF16)

    for copy in small[:3]:
        copy.wait()
    q = jnp.concatenate([q_buf[:, h * HD : (h + 1) * HD] for h in range(heads_here)], axis=0)
    scores = lax.dot_general(
        q, k_buf[...], (((1,), (1,)), ((), ())), preferred_element_type=F32
    ) / math.sqrt(HD)
    position = lax.rem(lax.broadcasted_iota(jnp.int32, scores.shape, 0), length)
    causal = position >= lax.broadcasted_iota(jnp.int32, scores.shape, 1)
    scores = jnp.where(causal, scores, -1e30)
    weights = jnp.exp(scores - jnp.max(scores, axis=-1, keepdims=True))
    probability = weights / jnp.sum(weights, axis=-1, keepdims=True)
    mixed = jnp.dot(probability.astype(BF16), v_buf[...], preferred_element_type=F32).astype(BF16)
    for k in range(chunks):
        for h in range(heads_here):
            at = h * HD % owned
            line[m, k, h * HD // owned, :, at : at + HD] = mixed[
                h * length + k * R : h * length + (k + 1) * R
            ]

    def line_copy(source, j, k, peer):
        block = line.at[source, k]
        return remote(block, block, line_s.at[0], line_r.at[k, j - 1], mp=peer)

    def line_send(k):
        for j in range(1, n):
            line_copy(m, j, k, lax.rem(m + j, n)).start()

    def spread_heads(k):
        for j in range(n):
            source = lax.rem(m + n - j, n)
            if j > 0:
                line_copy(source, j, k, source).wait_recv()
            for i in range(owners):
                owner = source * owners + i

                @pl.when(owner != b)
                def _(source=source, i=i, owner=owner):
                    remote(
                        line.at[source, k, i],
                        rows.at[k, my_slot],
                        owner_s.at[k],
                        owner_r.at[k],
                        batch=owner,
                    ).start()

                @pl.when(owner == b)
                def _(source=source, i=i):
                    rows[k, my_slot] = line[source, k, i]

    def all_owners(k):
        block = rows.at[k, pl.ds(0, nb - 1)]
        return remote(block, block, owner_s.at[k], owner_r.at[k], batch=mate)

    scatter_a = (part_a, near_a, mid_a, far_a, na_s, na_r, fa_s, fa_r)
    scatter_m = (part_m, near_m, mid_m, far_m, nm_s, nm_r, fm_s, fm_r)

    def near_copy(k, bufs):
        part, near, mid, far, near_s, near_r, far_s, far_r = bufs
        block = part.at[k, pl.ds((1 - core) * chips, chips)]
        return remote(block, near.at[k], near_s.at[0], near_r.at[k], batch=mate)

    def scatter_far(k, bufs):
        part, near, mid, far, near_s, near_r, far_s, far_r = bufs
        near_copy(k, bufs).wait_recv()
        for j in range(1, chips):
            target = lax.rem(chip + j, chips)
            mid[k, j - 1] = (
                part[k, core * chips + target].astype(F32) + near[k, target].astype(F32)
            ).astype(BF16)
            remote(
                mid.at[k, j - 1],
                far.at[k, j - 1],
                far_s.at[0],
                far_r.at[k],
                batch=2 * target + core,
            ).start()

    def scatter_total(k, bufs):
        part, near, mid, far, near_s, near_r, far_s, far_r = bufs
        total = part[k, my_slot].astype(F32) + near[k, chip].astype(F32)
        remote(mid.at[k], far.at[k], far_s.at[0], far_r.at[k], batch=mate).wait_recv()
        for j in range(1, chips):
            total = total + far[k, j - 1].astype(F32)
        return total

    def multiply_into(k, bufs, left, weight):
        tile = 512 if cols_d % 512 == 0 else cols_d

        def one(i, carry):
            at = pl.ds(pl.multiple_of(i * tile, tile), tile)
            made = jnp.dot(left(), weight[:, at], preferred_element_type=F32).astype(BF16)
            bufs[0][k, :, :, at] = made.reshape(nb, R, tile)
            return carry

        lax.fori_loop(0, cols_d // tile, one, 0)
        near_copy(k, bufs).start()

    def project(k):
        all_owners(k).wait_recv()

        @pl.when(k == 0)
        def _():
            load_wo.wait()

        x = rows[k].reshape(all_rows, owned)
        other = jnp.dot(pmat[...], x, preferred_element_type=F32)
        head = lax.broadcasted_iota(jnp.int32, (all_rows, owned), 1) // HD + b * (owned // HD)
        chosen = head == ablated_ref[0]
        for i in range(1, ablated_ref.shape[0]):
            chosen = chosen | (head == ablated_ref[i])
        x = jnp.where(chosen, other, x.astype(F32)).astype(BF16)
        multiply_into(k, scatter_a, lambda: x, wo_buf)

    def rows_at(k):
        return pl.ds(pl.multiple_of(k * R, R), R)

    def gather_far(k, j, source, peer):
        block = x_all.at[k, core * chips + source]
        return remote(block, block, agf_s.at[0], agf_r.at[k, j - 1], batch=peer)

    def gather_near(k, block):
        return remote(block, block, agn_s.at[0], agn_r.at[k], batch=mate)

    def gather_near_all(k):
        return gather_near(k, x_all.at[k, pl.ds((1 - core) * chips, chips)])

    def square_copy(k):
        place = lax.rem(m + n - end, n) - 1
        return remote(own_sq.at[k], got_sq.at[k, place], sq_s.at[0], sq_r.at[k], mp=end)

    def inverse_wait(k, count):
        block = inv.at[pl.ds(0, count)]
        return remote(block, block, inv_s.at[k], inv_r.at[k], batch=mate)

    def normalize(k):
        total = scatter_total(k, scatter_a)
        attn_ref[0, rows_at(k), :] = total.astype(BF16)
        state = res_buf[rows_at(k), :].astype(F32) + total
        x_all[k, my_slot] = (state * gain_ref[...].reshape(1, cols_d)).astype(BF16)
        for j in range(1, chips):
            gather_far(k, j, chip, 2 * lax.rem(chip + j, chips) + core).start()
        gather_near(k, x_all.at[k, my_slot]).start()
        squares = jnp.sum(state * state, axis=1, keepdims=True)
        own_sq[k] = jnp.broadcast_to(squares, (R, 128))

        @pl.when(m != end)
        def _():
            square_copy(k).start()

    def gather_rest(k):
        for j in range(1, chips):
            source = lax.rem(chip + chips - j, chips)
            gather_far(k, j, source, mate).wait_recv()
            gather_near(k, x_all.at[k, core * chips + source]).start()

        @pl.when(m == end)
        def _():
            total = own_sq[k]
            remote(got_sq.at[k], got_sq.at[k], sq_s.at[0], sq_r.at[k], mp=end).wait_recv()
            for j in range(1, n):
                total = total + got_sq[k, j - 1]
            mine = k * chips + chip
            inv[mine] = lax.rsqrt(total / D + 1e-05)
            for j in range(1, nb):
                remote(
                    inv.at[mine],
                    inv.at[mine],
                    inv_s.at[k],
                    inv_r.at[k],
                    batch=lax.rem(b + j, nb),
                ).start()

    pos_of = (m, n - 1 - m)
    way_of = (1, -1)

    def sum_copy(d, u, peer):
        at = lax.rem(u, reuse)
        return remote(own.at[d, u], got.at[d, u], sum_s.at[d], sum_r.at[d, at], mp=peer)

    def hid_copy(d, k, c, peer):
        block = hid.at[d, k, :, piece(c)]
        at = lax.rem(k * pieces + c, reuse)
        return remote(block, block, hid_s.at[d], hid_r.at[d, at], mp=peer)

    def unit(v):
        k, c = lax.div(v, slots), lax.rem(v, slots)
        return k, c, (v >= 0) & (v < chunks * slots) & (c < pieces)

    def step(i, carry):
        t = i - LEAD
        k, c, here = unit(t)

        @pl.when(here)
        def _():
            @pl.when(c == 0)
            def _():
                gather_near_all(k).wait_recv()

                @pl.when(k == 0)
                def _():
                    pltpu.make_async_copy(w_buf, w_buf, big_sem.at[2]).wait()

            x = x_all[k].reshape(all_rows, cols_d)
            u = k * pieces + c
            if joined:
                made = jnp.dot(x, w_buf[c], preferred_element_type=F32).astype(BF16)
                for d in range(2):
                    own[d, u] = made[d * half : (d + 1) * half]
            else:
                for which in range(2):
                    made = jnp.dot(x, w_buf[c, which], preferred_element_type=F32).astype(BF16)
                    for d in range(2):
                        own[d, u, which] = made[d * half : (d + 1) * half]

        for d in range(2):
            pos, way = pos_of[d], way_of[d]
            k, c, here = unit(t - LAG * pos)
            u = k * pieces + c

            @pl.when(here & (pos == 0))
            def _(d=d, u=u, way=way):
                sum_copy(d, u, m + way).start()

            @pl.when(here & (pos > 0) & (pos < n - 1))
            def _(d=d, u=u, way=way):
                sum_copy(d, u, m - way).wait_recv()
                own[d, u] = (own[d, u].astype(F32) + got[d, u].astype(F32)).astype(BF16)
                sum_copy(d, u, m + way).start()

            @pl.when(here & (pos == n - 1))
            def _(d=d, k=k, c=c, u=u, way=way):
                @pl.when(c == 0)
                def _():
                    @pl.when(core == d)
                    def _():
                        inverse_wait(k, chips - 1).wait_recv()

                    @pl.when(core != d)
                    def _():
                        inverse_wait(k, chips).wait_recv()

                sum_copy(d, u, m - way).wait_recv()
                inverse = inv[pl.ds(k * chips, chips)].reshape(half, 128)[:, :1]
                summed = own[d, u].astype(F32) + got[d, u].astype(F32)
                gate = (summed[:, :w] if joined else summed[0]) * inverse
                up = (summed[:, w:] if joined else summed[1]) * inverse
                hid[d, k, :, piece(c)] = (gate / (1.0 + jnp.exp(-gate)) * up).astype(BF16)
                hid_copy(d, k, c, m - way).start()

            k, c, here = unit(t - LAG * (2 * (n - 1) - pos))

            @pl.when(here & (pos < n - 1))
            def _(d=d, k=k, c=c, way=way, pos=pos):
                hid_copy(d, k, c, m + way).wait_recv()

                @pl.when(pos > 0)
                def _():
                    hid_copy(d, k, c, m - way).start()

        def stage(offset, first, do):
            v = t - offset
            k = lax.div(v, slots)

            @pl.when((v >= first * slots) & (k < chunks) & (lax.rem(v, slots) == 0))
            def _():
                do(k)

        done = pieces - 1 + LAG * 2 * (n - 1)

        def start_scatter(k):
            scatter_far(k, scatter_a)

            @pl.when(k == 0)
            def _():
                for later in range(2, chunks):
                    line_send(later)

        def down(k):
            @pl.when(k == 0)
            def _():
                load_wd.wait()

            multiply_into(
                k, scatter_m, lambda: hid[:, k].reshape(all_rows, pieces * w), wd_buf
            )

        def finish_rows(k):
            mlp_ref[0, rows_at(k), :] = scatter_total(k, scatter_m).astype(BF16)

        stage(done, 0, down)
        stage(done + 2, 0, lambda k: scatter_far(k, scatter_m))
        stage(done + 12, 0, finish_rows)
        stage(-LEAD, 0, project)
        stage(-16, 0, start_scatter)
        stage(-26, 1, spread_heads)
        stage(-8, 0, normalize)
        stage(-3, 0, gather_rest)
        return carry

    pl.semaphore_wait(barrier, n + nb - 2)
    line_send(0)
    spread_heads(0)
    if chunks > 1:
        line_send(1)
    small[3].wait()
    last = LEAD + (chunks - 1) * slots + pieces - 1 + LAG * 2 * (n - 1) + 12 + 1
    lax.fori_loop(0, last, step, 0)

    block = line.at[pl.ds(0, n - 1)]
    remote(block, block, line_s.at[0], line_r.at[0, 0], mp=end).wait_send()
    for k in range(chunks):
        all_owners(k).wait_send()
    for part, near, mid, far, near_s, near_r, far_s, far_r in (scatter_a, scatter_m):
        remote(near, near, near_s.at[0], near_r.at[0], batch=mate).wait_send()
        remote(mid, mid, far_s.at[0], far_r.at[0], batch=mate).wait_send()
    remote(mid_a, mid_a, agf_s.at[0], agf_r.at[0, 0], batch=mate).wait_send()
    remote(near_a, near_a, agn_s.at[0], agn_r.at[0], batch=mate).wait_send()

    @pl.when(m != end)
    def _():
        remote(own_sq, own_sq, sq_s.at[0], sq_r.at[0], mp=end).wait_send()

    @pl.when(m == end)
    def _():
        for k in range(chunks):
            inverse_wait(k, nb - 1).wait_send()

    for d in range(2):
        pos, way = pos_of[d], way_of[d]

        @pl.when(pos < n - 1)
        def _(d=d, way=way):
            remote(own.at[d], got.at[d], sum_s.at[d], sum_r.at[d, 0], mp=m + way).wait_send()

        @pl.when(pos > 0)
        def _(d=d, way=way):
            remote(hid.at[d], hid.at[d], hid_s.at[d], hid_r.at[d, 0], mp=m - way).wait_send()


def body(
    residual, query_states, key_states, value_states, prompt_perm, ablated_heads, out_weight,
    rms_gain, gate_weight, up_weight, down_weight,
):
    _, length, cols_d = residual.shape
    nb, n = lax.axis_size("batch"), lax.axis_size("mp")
    chips = nb // 2
    chunks = length // R
    owned = out_weight.shape[0]
    columns = query_states.shape[2]
    owners = columns // owned
    width = gate_weight.shape[1]
    joined = width % 128 == 0
    w = 128 if joined else width
    pieces = width // w
    slots = max(pieces, 14)
    units = chunks * pieces
    reuse = min(units, 2 * LAG * (n - 1) + 1)
    half = chips * R
    pair = (half, 2 * w) if joined else (2, half, w)
    vmem = pl.BlockSpec(memory_space=pltpu.VMEM)
    smem = pl.BlockSpec(memory_space=pltpu.SMEM)
    anywhere = pl.BlockSpec(memory_space=pl.ANY)
    dma = pltpu.SemaphoreType.DMA

    def scatter_bufs():
        return [
            pltpu.VMEM((chunks, nb, R, cols_d), BF16),
            pltpu.VMEM((chunks, chips, R, cols_d), BF16),
            pltpu.VMEM((chunks, chips - 1, R, cols_d), BF16),
            pltpu.VMEM((chunks, chips - 1, R, cols_d), BF16),
        ]

    out = jax.ShapeDtypeStruct((1, length, cols_d), BF16)
    return pl.pallas_call(
        functools.partial(layer_kernel, nb, n, slots, w, joined),
        in_specs=[smem, smem] + [anywhere] * 5 + [vmem] + [anywhere] * 3,
        out_specs=[vmem, vmem],
        out_shape=[out, out],
        scratch_shapes=[
            pltpu.VMEM((length, cols_d), BF16),
            pltpu.VMEM((length, columns), BF16),
            pltpu.VMEM((length, HD), BF16),
            pltpu.VMEM((length, HD), BF16),
            pltpu.VMEM((owned, cols_d), BF16),
            pltpu.VMEM((pieces, cols_d, 2 * w) if joined else (pieces, 2, cols_d, w), BF16),
            pltpu.VMEM((width, cols_d), BF16),
            pltpu.VMEM((nb * R, nb * R), BF16),
            pltpu.VMEM((n, chunks, owners, R, owned), BF16),
            pltpu.VMEM((chunks, nb, R, owned), BF16),
            *scatter_bufs(),
            *scatter_bufs(),
            pltpu.VMEM((chunks, nb, R, cols_d), BF16),
            pltpu.VMEM((chunks, R, 128), F32),
            pltpu.VMEM((chunks, n - 1, R, 128), F32),
            pltpu.VMEM((chunks * chips, R, 128), F32),
            pltpu.VMEM((2, units, *pair), BF16),
            pltpu.VMEM((2, units, *pair), BF16),
            pltpu.VMEM((2, chunks, half, width), BF16),
            dma((4,)),
            dma((3,)),
            dma((1,)),
            dma((chunks, n - 1)),
            dma((chunks,)),
            dma((chunks,)),
            *[dma((1,)), dma((chunks,)), dma((1,)), dma((chunks,))] * 2,
            dma((1,)),
            dma((chunks, chips - 1)),
            dma((1,)),
            dma((chunks,)),
            dma((1,)),
            dma((chunks,)),
            dma((chunks,)),
            dma((chunks,)),
            dma((2,)),
            dma((2, reuse)),
            dma((2,)),
            dma((2, reuse)),
        ],
        compiler_params=pltpu.CompilerParams(
            collective_id=1, has_side_effects=True, vmem_limit_bytes=VMEM
        ),
    )(
        prompt_perm, ablated_heads, residual, query_states, key_states, value_states, out_weight,
        rms_gain, gate_weight, up_weight, down_weight,
    )


def solution(mesh):
    placed = (
        P("batch", None, "mp"),
        P("batch", None, "mp"),
        P("batch", None, None),
        P("batch", None, None),
        P(),
        P(),
        P("batch", "mp"),
        P("mp"),
        P("mp", "batch"),
        P("mp", "batch"),
        P("batch", "mp"),
    )
    return jax.shard_map(
        body,
        mesh=mesh,
        in_specs=placed,
        out_specs=(P("batch", None, "mp"), P("batch", None, "mp")),
        check_vma=False,
    )
```

time: 147 us -> 123 us (0.84)
  Pallas kernels: 142 us -> 119 us
    pallas_call x1, Pallas kernels: 142 us -> 119 us  [body(): pl.pallas_call(functools.partial(layer_kernel, nb, n, slots, w, joined),...]
where the time goes in v2:
time: 123 us
  Pallas kernels  119 us (97%)
  local copies, waits for them, and re-layouts  3.34 us (3%)
    pallas_call x1, Pallas kernels, body(): pl.pallas_call(functools.partial(layer_kernel, nb, n, slots, w, joined),...  119 us
    unnamed x2, local copies, waits for them, and re-layouts  3.34 us

profile of v2, /device:TPU:0, one launch (start us, length us, event | category | flops | bytes accessed | tf_op | source)
XLA Modules:
  0.0 122.9 jit_solution(11468636210873942063)
XLA Ops:
  0.6 118.9 %shard_map.122 = (bf16[1,64,2048]{2,1,0:T(8,128)(2,1)}, bf16[1,64,2048]{2,1,0:T(8,128)(2,1)}) custom-call(s32[8]{0:T(128)} %perm_ref.1, s32[8]{0:T(128)} %ablated_ref.1, bf16[1,64,2048]{2,1,0:T(8,128)(2,1)} %res_hbm.1, bf16[1,64,1024]{2,1,0:T(8,128)(2,1)} %q_hbm.1, bf16[1,64,512]{2,1,0:T(8,128)(2,1)} %k_hbm.1, bf16[1,64,512]{2,1,0:T(8,128)(2,1)} %v_hbm.1, ...), custom_call_target="tpu_custom_call" | custom-call | tf_op jit(solution)/shard_map/pallas_call | solution.py:481
  119.6 1.7 %copy.15 = bf16[1,64,2048]{2,1,0:T(8,128)(2,1)} copy(bf16[1,64,2048]{2,1,0:T(8,128)(2,1)} %get-tuple-element.4) | data formatting | bytes 524288
  121.2 1.7 %copy.16 = bf16[1,64,2048]{2,1,0:T(8,128)(2,1)} copy(bf16[1,64,2048]{2,1,0:T(8,128)(2,1)} %get-tuple-element.5) | data formatting | bytes 524288

commit v3 on v2

--- a/solution.py
+++ b/solution.py
@@ -13,8 +13,10 @@
 KV = 4
 HD = 128
 R = 16
-LAG = 3
+LAG = 4
+HLAG = 4
 LEAD = 20
+FINISH = 12
 VMEM = 60 * 2**20
 BF16, F32 = jnp.bfloat16, jnp.float32
 
@@ -33,12 +35,12 @@
 def layer_kernel(
     nb, n, slots, w, joined,
     perm_ref, ablated_ref, res_hbm, q_hbm, k_hbm, v_hbm, wo_hbm, gain_ref, wg_hbm, wu_hbm, wd_hbm,
-    attn_ref, mlp_ref,
-    res_buf, q_buf, k_buf, v_buf, wo_buf, w_buf, wd_buf,
-    pmat, line, rows,
+    attn_hbm, mlp_hbm,
+    attn_buf, mlp_buf, res_buf, q_buf, k_buf, v_buf, wo_buf, w_buf, wd_buf,
+    pmat, line, rows, swapped,
     part_a, near_a, mid_a, far_a, part_m, near_m, mid_m, far_m,
     x_all, own_sq, got_sq, inv, own, got, hid,
-    small_sem, big_sem,
+    small_sem, big_sem, out_sem,
     line_s, line_r, owner_s, owner_r,
     na_s, na_r, fa_s, fa_r, nm_s, nm_r, fm_s, fm_r,
     agf_s, agf_r, agn_s, agn_r, sq_s, sq_r, inv_s, inv_r, sum_s, sum_r, hid_s, hid_r,
@@ -190,19 +192,17 @@
             total = total + far[k, j - 1].astype(F32)
         return total
 
-    def multiply_into(k, bufs, left, weight):
-        tile = 512 if cols_d % 512 == 0 else cols_d
-
-        def one(i, carry):
-            at = pl.ds(pl.multiple_of(i * tile, tile), tile)
-            made = jnp.dot(left(), weight[:, at], preferred_element_type=F32).astype(BF16)
-            bufs[0][k, :, :, at] = made.reshape(nb, R, tile)
-            return carry
-
-        lax.fori_loop(0, cols_d // tile, one, 0)
-        near_copy(k, bufs).start()
-
-    def project(k):
+    tile = 512 if cols_d % 512 == 0 else cols_d
+    tiles = cols_d // tile
+
+    def multiply_tile(k, bufs, left, weight, i):
+        at = pl.ds(i * tile, tile)
+        made = jnp.dot(left, weight[:, at], preferred_element_type=F32).astype(BF16)
+        bufs[0][k, :, :, at] = made.reshape(nb, R, tile)
+        if i == tiles - 1:
+            near_copy(k, bufs).start()
+
+    def swap(k):
         all_owners(k).wait_recv()
 
         @pl.when(k == 0)
@@ -215,11 +215,18 @@
         chosen = head == ablated_ref[0]
         for i in range(1, ablated_ref.shape[0]):
             chosen = chosen | (head == ablated_ref[i])
-        x = jnp.where(chosen, other, x.astype(F32)).astype(BF16)
-        multiply_into(k, scatter_a, lambda: x, wo_buf)
+        swapped[...] = jnp.where(chosen, other, x.astype(F32)).astype(BF16)
+
+    def project(i, k):
+        multiply_tile(k, scatter_a, swapped[...], wo_buf, i)
 
     def rows_at(k):
         return pl.ds(pl.multiple_of(k * R, R), R)
+
+    def out_copy(buf, hbm, k, which):
+        return pltpu.make_async_copy(
+            buf.at[rows_at(k), :], hbm.at[0, rows_at(k), :], out_sem.at[which]
+        )
 
     def gather_far(k, j, source, peer):
         block = x_all.at[k, core * chips + source]
@@ -241,7 +248,8 @@
 
     def normalize(k):
         total = scatter_total(k, scatter_a)
-        attn_ref[0, rows_at(k), :] = total.astype(BF16)
+        attn_buf[rows_at(k), :] = total.astype(BF16)
+        out_copy(attn_buf, attn_hbm, k, 0).start()
         state = res_buf[rows_at(k), :].astype(F32) + total
         x_all[k, my_slot] = (state * gain_ref[...].reshape(1, cols_d)).astype(BF16)
         for j in range(1, chips):
@@ -284,18 +292,26 @@
         at = lax.rem(u, reuse)
         return remote(own.at[d, u], got.at[d, u], sum_s.at[d], sum_r.at[d, at], mp=peer)
 
-    def hid_copy(d, k, c, peer):
-        block = hid.at[d, k, :, piece(c)]
-        at = lax.rem(k * pieces + c, reuse)
+    def hid_copy(d, u, peer):
+        block = hid.at[d, u]
+        at = lax.rem(u, reuse)
         return remote(block, block, hid_s.at[d], hid_r.at[d, at], mp=peer)
 
-    def unit(v):
-        k, c = lax.div(v, slots), lax.rem(v, slots)
-        return k, c, (v >= 0) & (v < chunks * slots) & (c < pieces)
-
-    def step(i, carry):
-        t = i - LEAD
-        k, c, here = unit(t)
+    def cut(offset):
+        return lax.div(offset, slots), lax.rem(offset, slots)
+
+    made_cut = cut(jnp.int32(LEAD))
+    sum_cut = [cut(LEAD + LAG * pos_of[d]) for d in range(2)]
+    back_cut = [cut(LEAD + LAG * (n - 1) + HLAG * (n - 1 - pos_of[d])) for d in range(2)]
+
+    def step(window, s):
+        def unit(offset):
+            q, r = offset
+            late = (s < r).astype(jnp.int32)
+            k, c = window - q - late, s - r + slots * late
+            return k, c, (k >= 0) & (k < chunks) & (c < pieces)
+
+        k, c, here = unit(made_cut)
 
         @pl.when(here)
         def _():
@@ -321,7 +337,7 @@
 
         for d in range(2):
             pos, way = pos_of[d], way_of[d]
-            k, c, here = unit(t - LAG * pos)
+            k, c, here = unit(sum_cut[d])
             u = k * pieces + c
 
             @pl.when(here & (pos == 0))
@@ -351,28 +367,27 @@
                 summed = own[d, u].astype(F32) + got[d, u].astype(F32)
                 gate = (summed[:, :w] if joined else summed[0]) * inverse
                 up = (summed[:, w:] if joined else summed[1]) * inverse
-                hid[d, k, :, piece(c)] = (gate / (1.0 + jnp.exp(-gate)) * up).astype(BF16)
-                hid_copy(d, k, c, m - way).start()
-
-            k, c, here = unit(t - LAG * (2 * (n - 1) - pos))
+                hid[d, u] = (gate / (1.0 + jnp.exp(-gate)) * up).astype(BF16)
+                hid_copy(d, u, m - way).start()
+
+            k, c, here = unit(back_cut[d])
+            u = k * pieces + c
 
             @pl.when(here & (pos < n - 1))
-            def _(d=d, k=k, c=c, way=way, pos=pos):
-                hid_copy(d, k, c, m + way).wait_recv()
+            def _(d=d, u=u, way=way, pos=pos):
+                hid_copy(d, u, m + way).wait_recv()
 
                 @pl.when(pos > 0)
                 def _():
-                    hid_copy(d, k, c, m - way).start()
+                    hid_copy(d, u, m - way).start()
 
         def stage(offset, first, do):
-            v = t - offset
-            k = lax.div(v, slots)
-
-            @pl.when((v >= first * slots) & (k < chunks) & (lax.rem(v, slots) == 0))
+            q, r = divmod(LEAD + offset, slots)
+            k = window - q
+
+            @pl.when((s == r) & (k >= first) & (k < chunks))
             def _():
                 do(k)
-
-        done = pieces - 1 + LAG * 2 * (n - 1)
 
         def start_scatter(k):
             scatter_far(k, scatter_a)
@@ -382,37 +397,55 @@
                 for later in range(2, chunks):
                     line_send(later)
 
-        def down(k):
-            @pl.when(k == 0)
-            def _():
-                load_wd.wait()
-
-            multiply_into(
-                k, scatter_m, lambda: hid[:, k].reshape(all_rows, pieces * w), wd_buf
-            )
+        def down(i, k):
+            if i == 0:
+
+                @pl.when(k == 0)
+                def _():
+                    load_wd.wait()
+
+            left = [
+                jnp.concatenate([hid[d, k * pieces + c] for c in range(pieces)], axis=1)
+                for d in range(2)
+            ]
+            multiply_tile(k, scatter_m, jnp.concatenate(left, axis=0), wd_buf, i)
 
         def finish_rows(k):
-            mlp_ref[0, rows_at(k), :] = scatter_total(k, scatter_m).astype(BF16)
-
-        stage(done, 0, down)
-        stage(done + 2, 0, lambda k: scatter_far(k, scatter_m))
-        stage(done + 12, 0, finish_rows)
-        stage(-LEAD, 0, project)
-        stage(-16, 0, start_scatter)
+            mlp_buf[rows_at(k), :] = scatter_total(k, scatter_m).astype(BF16)
+            out_copy(mlp_buf, mlp_hbm, k, 1).start()
+
+        for i in range(tiles):
+            stage(done + i, 0, functools.partial(down, i))
+        stage(done + tiles + 1, 0, lambda k: scatter_far(k, scatter_m))
+        stage(done + FINISH, 0, finish_rows)
+        stage(-LEAD, 0, swap)
+        for i in range(tiles):
+            stage(-LEAD + (i * 4) // tiles, 0, functools.partial(project, i))
+        stage(-15, 0, start_scatter)
         stage(-26, 1, spread_heads)
         stage(-8, 0, normalize)
         stage(-3, 0, gather_rest)
-        return carry
-
+
+    done = pieces - 1 + LAG * (n - 1) + HLAG * (n - 1)
     pl.semaphore_wait(barrier, n + nb - 2)
     line_send(0)
     spread_heads(0)
     if chunks > 1:
         line_send(1)
     small[3].wait()
-    last = LEAD + (chunks - 1) * slots + pieces - 1 + LAG * 2 * (n - 1) + 12 + 1
-    lax.fori_loop(0, last, step, 0)
-
+    last = LEAD + (chunks - 1) * slots + done + FINISH + 1
+
+    def window_steps(window, carry):
+        def one(s, carry):
+            step(window, s)
+            return carry
+
+        return lax.fori_loop(0, slots, one, carry)
+
+    lax.fori_loop(0, -(-last // slots), window_steps, 0)
+
+    pltpu.make_async_copy(attn_buf, attn_hbm.at[0], out_sem.at[0]).wait()
+    pltpu.make_async_copy(mlp_buf, mlp_hbm.at[0], out_sem.at[1]).wait()
     block = line.at[pl.ds(0, n - 1)]
     remote(block, block, line_s.at[0], line_r.at[0, 0], mp=end).wait_send()
     for k in range(chunks):
@@ -461,7 +494,7 @@
     pieces = width // w
     slots = max(pieces, 14)
     units = chunks * pieces
-    reuse = min(units, 2 * LAG * (n - 1) + 1)
+    reuse = min(units, (LAG + HLAG) * (n - 1) + 1)
     half = chips * R
     pair = (half, 2 * w) if joined else (2, half, w)
     vmem = pl.BlockSpec(memory_space=pltpu.VMEM)
@@ -478,12 +511,14 @@
         ]
 
     out = jax.ShapeDtypeStruct((1, length, cols_d), BF16)
-    return pl.pallas_call(
+    attn, mlp = pl.pallas_call(
         functools.partial(layer_kernel, nb, n, slots, w, joined),
         in_specs=[smem, smem] + [anywhere] * 5 + [vmem] + [anywhere] * 3,
-        out_specs=[vmem, vmem],
+        out_specs=[anywhere, anywhere],
         out_shape=[out, out],
         scratch_shapes=[
+            pltpu.VMEM((length, cols_d), BF16),
+            pltpu.VMEM((length, cols_d), BF16),
             pltpu.VMEM((length, cols_d), BF16),
             pltpu.VMEM((length, columns), BF16),
             pltpu.VMEM((length, HD), BF16),
@@ -494,6 +529,7 @@
             pltpu.VMEM((nb * R, nb * R), BF16),
             pltpu.VMEM((n, chunks, owners, R, owned), BF16),
             pltpu.VMEM((chunks, nb, R, owned), BF16),
+            pltpu.VMEM((nb * R, owned), BF16),
             *scatter_bufs(),
             *scatter_bufs(),
             pltpu.VMEM((chunks, nb, R, cols_d), BF16),
@@ -502,9 +538,10 @@
             pltpu.VMEM((chunks * chips, R, 128), F32),
             pltpu.VMEM((2, units, *pair), BF16),
             pltpu.VMEM((2, units, *pair), BF16),
-            pltpu.VMEM((2, chunks, half, width), BF16),
+            pltpu.VMEM((2, units, half, w), BF16),
             dma((4,)),
             dma((3,)),
+            dma((2,)),
             dma((1,)),
             dma((chunks, n - 1)),
             dma((chunks,)),
@@ -530,6 +567,35 @@
         prompt_perm, ablated_heads, residual, query_states, key_states, value_states, out_weight,
         rms_gain, gate_weight, up_weight, down_weight,
     )
+    return pl.pallas_call(
+        place_kernel,
+        in_specs=[anywhere, anywhere],
+        out_specs=[anywhere, anywhere],
+        out_shape=[out, out],
+        scratch_shapes=[pltpu.VMEM(out.shape, BF16), pltpu.VMEM(out.shape, BF16), dma((2, 2, 2))],
+    )(attn, mlp)
+
+
+def place_kernel(attn_ref, mlp_ref, attn_out, mlp_out, attn_buf, mlp_buf, sem):
+    rows = attn_ref.shape[1] // 2
+    pairs = ((attn_ref, attn_buf, attn_out), (mlp_ref, mlp_buf, mlp_out))
+    moves = [(i, j, pl.ds(j * rows, rows)) for j in range(2) for i in range(2)]
+
+    def load(i, j, at):
+        src, buf, dst = pairs[i]
+        return pltpu.make_async_copy(src.at[:, at], buf.at[:, at], sem.at[0, i, j])
+
+    def store(i, j, at):
+        src, buf, dst = pairs[i]
+        return pltpu.make_async_copy(buf.at[:, at], dst.at[:, at], sem.at[1, i, j])
+
+    for move in moves:
+        load(*move).start()
+    for move in moves:
+        load(*move).wait()
+        store(*move).start()
+    for move in moves:
+        store(*move).wait()
 
 
 def solution(mesh):

time: 123 us -> 116 us (0.943)
  Pallas kernels: 119 us -> 115 us
  local copies, waits for them, and re-layouts: 3.34 us -> 0 us
    pallas_call x1, Pallas kernels: 119 us -> 113 us  [body(): pl.pallas_call(functools.partial(layer_kernel, nb, n, slots, w, joined),...]
    unnamed x2 -> x0, local copies, waits for them, and re-layouts: 3.34 us -> none
    pallas_call x0 -> x1, Pallas kernels: none -> 1.82 us  [body(): pl.pallas_call(place_kernel, in_specs=[anywhere, anywhere], out_specs=[an...]
where the time goes in v3:
time: 116 us; the launch traced here: 115 us
  Pallas kernels  115 us (99%)
    pallas_call x1, Pallas kernels, body(): pl.pallas_call(functools.partial(layer_kernel, nb, n, slots, w, joined),...  113 us

profile of v3, /device:TPU:0, one launch (start us, length us, event | category | flops | bytes accessed | tf_op | source)
XLA Modules:
  0.0 115.4 jit_solution(12486024297538526998)
XLA Ops:
  0.6 113.0 %shard_map.122 = (bf16[1,64,2048]{2,1,0:T(8,128)(2,1)}, bf16[1,64,2048]{2,1,0:T(8,128)(2,1)}) custom-call(s32[8]{0:T(128)} %perm_ref.1, s32[8]{0:T(128)} %ablated_ref.1, bf16[1,64,2048]{2,1,0:T(8,128)(2,1)} %res_hbm.1, bf16[1,64,1024]{2,1,0:T(8,128)(2,1)} %q_hbm.1, bf16[1,64,512]{2,1,0:T(8,128)(2,1)} %k_hbm.1, bf16[1,64,512]{2,1,0:T(8,128)(2,1)} %v_hbm.1, ...), custom_call_target="tpu_custom_call" | custom-call | tf_op jit(solution)/shard_map/pallas_call | solution.py:514
  113.6 1.8 %shard_map.123 = (bf16[1,64,2048]{2,1,0:T(8,128)(2,1)}, bf16[1,64,2048]{2,1,0:T(8,128)(2,1)}) custom-call(bf16[1,64,2048]{2,1,0:T(8,128)(2,1)} %get-tuple-element.4.attn_ref, bf16[1,64,2048]{2,1,0:T(8,128)(2,1)} %get-tuple-element.5.mlp_ref), custom_call_target="tpu_custom_call" | custom-call | tf_op jit(solution)/shard_map/pallas_call | solution.py:570

commit v4 on v3

--- a/solution.py
+++ b/solution.py
@@ -17,6 +17,7 @@
 HLAG = 4
 LEAD = 20
 FINISH = 12
+DIRECT = 6
 VMEM = 60 * 2**20
 BF16, F32 = jnp.bfloat16, jnp.float32
 
@@ -55,6 +56,8 @@
     _, _, owners, _, owned = line.shape
     pieces = w_buf.shape[0]
     reuse = sum_r.shape[1]
+    units = chunks * pieces
+    direct = min(DIRECT, units // (n - 1))
     half = chips * R
     all_rows = nb * R
     heads_here = q_buf.shape[1] // HD
@@ -163,44 +166,53 @@
     scatter_a = (part_a, near_a, mid_a, far_a, na_s, na_r, fa_s, fa_r)
     scatter_m = (part_m, near_m, mid_m, far_m, nm_s, nm_r, fm_s, fm_r)
 
-    def near_copy(k, bufs):
+    part_cols = [pl.ds(h * cols_d // 2, cols_d // 2) for h in range(2)]
+
+    def near_copy(k, h, bufs):
         part, near, mid, far, near_s, near_r, far_s, far_r = bufs
-        block = part.at[k, pl.ds((1 - core) * chips, chips)]
-        return remote(block, near.at[k], near_s.at[0], near_r.at[k], batch=mate)
-
-    def scatter_far(k, bufs):
+        block = part.at[k, pl.ds((1 - core) * chips, chips), :, part_cols[h]]
+        return remote(
+            block, near.at[k, :, :, part_cols[h]], near_s.at[0], near_r.at[k, h], batch=mate
+        )
+
+    def scatter_far(h, bufs, k):
         part, near, mid, far, near_s, near_r, far_s, far_r = bufs
-        near_copy(k, bufs).wait_recv()
+        near_copy(k, h, bufs).wait_recv()
+        at = part_cols[h]
         for j in range(1, chips):
             target = lax.rem(chip + j, chips)
-            mid[k, j - 1] = (
-                part[k, core * chips + target].astype(F32) + near[k, target].astype(F32)
+            mid[k, j - 1, :, at] = (
+                part[k, core * chips + target, :, at].astype(F32)
+                + near[k, target, :, at].astype(F32)
             ).astype(BF16)
             remote(
-                mid.at[k, j - 1],
-                far.at[k, j - 1],
+                mid.at[k, j - 1, :, at],
+                far.at[k, j - 1, :, at],
                 far_s.at[0],
-                far_r.at[k],
+                far_r.at[k, h],
                 batch=2 * target + core,
             ).start()
 
-    def scatter_total(k, bufs):
+    def scatter_total(k, h, bufs):
         part, near, mid, far, near_s, near_r, far_s, far_r = bufs
-        total = part[k, my_slot].astype(F32) + near[k, chip].astype(F32)
-        remote(mid.at[k], far.at[k], far_s.at[0], far_r.at[k], batch=mate).wait_recv()
+        at = part_cols[h]
+        total = part[k, my_slot, :, at].astype(F32) + near[k, chip, :, at].astype(F32)
+        remote(
+            mid.at[k, :, :, at], far.at[k, :, :, at], far_s.at[0], far_r.at[k, h], batch=mate
+        ).wait_recv()
         for j in range(1, chips):
-            total = total + far[k, j - 1].astype(F32)
+            total = total + far[k, j - 1, :, at].astype(F32)
         return total
 
-    tile = 512 if cols_d % 512 == 0 else cols_d
-    tiles = cols_d // tile
-
-    def multiply_tile(k, bufs, left, weight, i):
-        at = pl.ds(i * tile, tile)
-        made = jnp.dot(left, weight[:, at], preferred_element_type=F32).astype(BF16)
-        bufs[0][k, :, :, at] = made.reshape(nb, R, tile)
-        if i == tiles - 1:
-            near_copy(k, bufs).start()
+    tile = 512 if cols_d % 1024 == 0 else cols_d // 2
+    tiles = cols_d // tile // 2
+
+    def multiply_half(k, h, bufs, left, weight):
+        for i in range(h * tiles, (h + 1) * tiles):
+            at = pl.ds(i * tile, tile)
+            made = jnp.dot(left, weight[:, at], preferred_element_type=F32).astype(BF16)
+            bufs[0][k, :, :, at] = made.reshape(nb, R, tile)
+        near_copy(k, h, bufs).start()
 
     def swap(k):
         all_owners(k).wait_recv()
@@ -217,8 +229,8 @@
             chosen = chosen | (head == ablated_ref[i])
         swapped[...] = jnp.where(chosen, other, x.astype(F32)).astype(BF16)
 
-    def project(i, k):
-        multiply_tile(k, scatter_a, swapped[...], wo_buf, i)
+    def project(h, k):
+        multiply_half(k, h, scatter_a, swapped[...], wo_buf)
 
     def rows_at(k):
         return pl.ds(pl.multiple_of(k * R, R), R)
@@ -228,15 +240,13 @@
             buf.at[rows_at(k), :], hbm.at[0, rows_at(k), :], out_sem.at[which]
         )
 
-    def gather_far(k, j, source, peer):
-        block = x_all.at[k, core * chips + source]
-        return remote(block, block, agf_s.at[0], agf_r.at[k, j - 1], batch=peer)
-
-    def gather_near(k, block):
-        return remote(block, block, agn_s.at[0], agn_r.at[k], batch=mate)
-
-    def gather_near_all(k):
-        return gather_near(k, x_all.at[k, pl.ds((1 - core) * chips, chips)])
+    def gather_far(k, h, j, source, peer):
+        block = x_all.at[k, core * chips + source, :, part_cols[h]]
+        return remote(block, block, agf_s.at[0], agf_r.at[k, j - 1, h], batch=peer)
+
+    def gather_near(k, h, slots):
+        block = x_all.at[k, slots, :, part_cols[h]]
+        return remote(block, block, agn_s.at[0], agn_r.at[k, h], batch=mate)
 
     def square_copy(k):
         place = lax.rem(m + n - end, n) - 1
@@ -246,27 +256,33 @@
         block = inv.at[pl.ds(0, count)]
         return remote(block, block, inv_s.at[k], inv_r.at[k], batch=mate)
 
-    def normalize(k):
-        total = scatter_total(k, scatter_a)
-        attn_buf[rows_at(k), :] = total.astype(BF16)
+    def normalize(h, k):
+        at = part_cols[h]
+        total = scatter_total(k, h, scatter_a)
+        attn_buf[rows_at(k), at] = total.astype(BF16)
+        state = res_buf[rows_at(k), at].astype(F32) + total
+        x_all[k, my_slot, :, at] = (state * gain_ref[at].reshape(1, cols_d // 2)).astype(BF16)
+        for j in range(1, chips):
+            gather_far(k, h, j, chip, 2 * lax.rem(chip + j, chips) + core).start()
+        gather_near(k, h, my_slot).start()
+        squares = jnp.broadcast_to(jnp.sum(state * state, axis=1, keepdims=True), (R, 128))
+        if h == 0:
+            own_sq[k] = squares
+            return
+        own_sq[k] = own_sq[k] + squares
         out_copy(attn_buf, attn_hbm, k, 0).start()
-        state = res_buf[rows_at(k), :].astype(F32) + total
-        x_all[k, my_slot] = (state * gain_ref[...].reshape(1, cols_d)).astype(BF16)
-        for j in range(1, chips):
-            gather_far(k, j, chip, 2 * lax.rem(chip + j, chips) + core).start()
-        gather_near(k, x_all.at[k, my_slot]).start()
-        squares = jnp.sum(state * state, axis=1, keepdims=True)
-        own_sq[k] = jnp.broadcast_to(squares, (R, 128))
 
         @pl.when(m != end)
         def _():
             square_copy(k).start()
 
-    def gather_rest(k):
+    def gather_rest(h, k):
         for j in range(1, chips):
             source = lax.rem(chip + chips - j, chips)
-            gather_far(k, j, source, mate).wait_recv()
-            gather_near(k, x_all.at[k, core * chips + source]).start()
+            gather_far(k, h, j, source, mate).wait_recv()
+            gather_near(k, h, core * chips + source).start()
+        if h == 0:
+            return
 
         @pl.when(m == end)
         def _():
@@ -297,6 +313,11 @@
         at = lax.rem(u, reuse)
         return remote(block, block, hid_s.at[d], hid_r.at[d, at], mp=peer)
 
+    def hid_direct(d, u, peer):
+        block = hid.at[d, u]
+        at = lax.rem(u, reuse)
+        return remote(block, block, hid_s.at[2 + d], hid_r.at[d, at], mp=peer)
+
     def cut(offset):
         return lax.div(offset, slots), lax.rem(offset, slots)
 
@@ -317,7 +338,8 @@
         def _():
             @pl.when(c == 0)
             def _():
-                gather_near_all(k).wait_recv()
+                for h in range(2):
+                    gather_near(k, h, pl.ds((1 - core) * chips, chips)).wait_recv()
 
                 @pl.when(k == 0)
                 def _():
@@ -368,7 +390,15 @@
                 gate = (summed[:, :w] if joined else summed[0]) * inverse
                 up = (summed[:, w:] if joined else summed[1]) * inverse
                 hid[d, u] = (gate / (1.0 + jnp.exp(-gate)) * up).astype(BF16)
-                hid_copy(d, u, m - way).start()
+
+                @pl.when(u < units - direct)
+                def _():
+                    hid_copy(d, u, m - way).start()
+
+                @pl.when(u >= units - direct)
+                def _():
+                    for j in range(1, n):
+                        hid_direct(d, u, m - way * j).start()
 
             k, c, here = unit(back_cut[d])
             u = k * pieces + c
@@ -377,7 +407,7 @@
             def _(d=d, u=u, way=way, pos=pos):
                 hid_copy(d, u, m + way).wait_recv()
 
-                @pl.when(pos > 0)
+                @pl.when((pos > 0) & (u < units - direct))
                 def _():
                     hid_copy(d, u, m - way).start()
 
@@ -390,15 +420,15 @@
                 do(k)
 
         def start_scatter(k):
-            scatter_far(k, scatter_a)
+            scatter_far(1, scatter_a, k)
 
             @pl.when(k == 0)
             def _():
                 for later in range(2, chunks):
                     line_send(later)
 
-        def down(i, k):
-            if i == 0:
+        def down(h, k):
+            if h == 0:
 
                 @pl.when(k == 0)
                 def _():
@@ -408,23 +438,29 @@
                 jnp.concatenate([hid[d, k * pieces + c] for c in range(pieces)], axis=1)
                 for d in range(2)
             ]
-            multiply_tile(k, scatter_m, jnp.concatenate(left, axis=0), wd_buf, i)
-
-        def finish_rows(k):
-            mlp_buf[rows_at(k), :] = scatter_total(k, scatter_m).astype(BF16)
-            out_copy(mlp_buf, mlp_hbm, k, 1).start()
-
-        for i in range(tiles):
-            stage(done + i, 0, functools.partial(down, i))
-        stage(done + tiles + 1, 0, lambda k: scatter_far(k, scatter_m))
-        stage(done + FINISH, 0, finish_rows)
+            multiply_half(k, h, scatter_m, jnp.concatenate(left, axis=0), wd_buf)
+
+        def finish_rows(h, k):
+            mlp_buf[rows_at(k), part_cols[h]] = scatter_total(k, h, scatter_m).astype(BF16)
+            if h == 1:
+                out_copy(mlp_buf, mlp_hbm, k, 1).start()
+
+        for h in range(2):
+            stage(done + h, 0, functools.partial(down, h))
+        for h in range(2):
+            stage(done + 2 + h, 0, functools.partial(scatter_far, h, scatter_m))
+        for h in range(2):
+            stage(done + FINISH - 1 + h, 0, functools.partial(finish_rows, h))
         stage(-LEAD, 0, swap)
-        for i in range(tiles):
-            stage(-LEAD + (i * 4) // tiles, 0, functools.partial(project, i))
-        stage(-15, 0, start_scatter)
+        for h in range(2):
+            stage(-LEAD + h, 0, functools.partial(project, h))
+        stage(-17, 0, functools.partial(scatter_far, 0, scatter_a))
+        stage(-16, 0, start_scatter)
         stage(-26, 1, spread_heads)
-        stage(-8, 0, normalize)
-        stage(-3, 0, gather_rest)
+        for h in range(2):
+            stage(-8 + h, 0, functools.partial(normalize, h))
+        for h in range(2):
+            stage(-2 + h, 0, functools.partial(gather_rest, h))
 
     done = pieces - 1 + LAG * (n - 1) + HLAG * (n - 1)
     pl.semaphore_wait(barrier, n + nb - 2)
@@ -451,10 +487,10 @@
     for k in range(chunks):
         all_owners(k).wait_send()
     for part, near, mid, far, near_s, near_r, far_s, far_r in (scatter_a, scatter_m):
-        remote(near, near, near_s.at[0], near_r.at[0], batch=mate).wait_send()
-        remote(mid, mid, far_s.at[0], far_r.at[0], batch=mate).wait_send()
-    remote(mid_a, mid_a, agf_s.at[0], agf_r.at[0, 0], batch=mate).wait_send()
-    remote(near_a, near_a, agn_s.at[0], agn_r.at[0], batch=mate).wait_send()
+        remote(near, near, near_s.at[0], near_r.at[0, 0], batch=mate).wait_send()
+        remote(mid, mid, far_s.at[0], far_r.at[0, 0], batch=mate).wait_send()
+    remote(mid_a, mid_a, agf_s.at[0], agf_r.at[0, 0, 0], batch=mate).wait_send()
+    remote(near_a, near_a, agn_s.at[0], agn_r.at[0, 0], batch=mate).wait_send()
 
     @pl.when(m != end)
     def _():
@@ -474,7 +510,15 @@
 
         @pl.when(pos > 0)
         def _(d=d, way=way):
-            remote(hid.at[d], hid.at[d], hid_s.at[d], hid_r.at[d, 0], mp=m - way).wait_send()
+            block = hid.at[d, pl.ds(0, units - direct)]
+            remote(block, block, hid_s.at[d], hid_r.at[d, 0], mp=m - way).wait_send()
+
+        if direct:
+
+            @pl.when(pos == n - 1)
+            def _(d=d, way=way):
+                block = hid.at[d, pl.ds(0, direct * (n - 1))]
+                remote(block, block, hid_s.at[2 + d], hid_r.at[d, 0], mp=m - way).wait_send()
 
 
 def body(
@@ -546,18 +590,18 @@
             dma((chunks, n - 1)),
             dma((chunks,)),
             dma((chunks,)),
-            *[dma((1,)), dma((chunks,)), dma((1,)), dma((chunks,))] * 2,
+            *[dma((1,)), dma((chunks, 2))] * 4,
             dma((1,)),
-            dma((chunks, chips - 1)),
+            dma((chunks, chips - 1, 2)),
             dma((1,)),
-            dma((chunks,)),
+            dma((chunks, 2)),
             dma((1,)),
             dma((chunks,)),
             dma((chunks,)),
             dma((chunks,)),
             dma((2,)),
             dma((2, reuse)),
-            dma((2,)),
+            dma((4,)),
             dma((2, reuse)),
         ],
         compiler_params=pltpu.CompilerParams(

time: 116 us -> 112 us (0.966)
  Pallas kernels: 115 us -> 111 us
    pallas_call x1, Pallas kernels: 113 us -> 110 us  [body(): pl.pallas_call(functools.partial(layer_kernel, nb, n, slots, w, joined),...]
where the time goes in v4:
time: 112 us
  Pallas kernels  111 us (99%)
    pallas_call x1, Pallas kernels, body(): pl.pallas_call(functools.partial(layer_kernel, nb, n, slots, w, joined),...  110 us

profile of v4, /device:TPU:0, one launch (start us, length us, event | category | flops | bytes accessed | tf_op | source)
XLA Modules:
  0.0 112.0 jit_solution(10373293340559437003)
XLA Ops:
  0.6 109.6 %shard_map.122 = (bf16[1,64,2048]{2,1,0:T(8,128)(2,1)}, bf16[1,64,2048]{2,1,0:T(8,128)(2,1)}) custom-call(s32[8]{0:T(128)} %perm_ref.1, s32[8]{0:T(128)} %ablated_ref.1, bf16[1,64,2048]{2,1,0:T(8,128)(2,1)} %res_hbm.1, bf16[1,64,1024]{2,1,0:T(8,128)(2,1)} %q_hbm.1, bf16[1,64,512]{2,1,0:T(8,128)(2,1)} %k_hbm.1, bf16[1,64,512]{2,1,0:T(8,128)(2,1)} %v_hbm.1, ...), custom_call_target="tpu_custom_call" | custom-call | tf_op jit(solution)/shard_map/pallas_call | solution.py:558
  110.2 1.8 %shard_map.123 = (bf16[1,64,2048]{2,1,0:T(8,128)(2,1)}, bf16[1,64,2048]{2,1,0:T(8,128)(2,1)}) custom-call(bf16[1,64,2048]{2,1,0:T(8,128)(2,1)} %get-tuple-element.4.attn_ref, bf16[1,64,2048]{2,1,0:T(8,128)(2,1)} %get-tuple-element.5.mlp_ref), custom_call_target="tpu_custom_call" | custom-call | tf_op jit(solution)/shard_map/pallas_call | solution.py:614

commit v5 on v4

--- a/solution.py
+++ b/solution.py
@@ -17,7 +17,7 @@
 HLAG = 4
 LEAD = 20
 FINISH = 12
-DIRECT = 6
+DIRECT = 3
 VMEM = 60 * 2**20
 BF16, F32 = jnp.bfloat16, jnp.float32
 

time: 112 us -> 111 us (level)
  no operation moved by 1% of the time
where the time goes in v5:
time: 111 us
  Pallas kernels  111 us (100%)
    pallas_call x1, Pallas kernels, body(): pl.pallas_call(functools.partial(layer_kernel, nb, n, slots, w, joined),...  109 us

profile of v5, /device:TPU:0, one launch (start us, length us, event | category | flops | bytes accessed | tf_op | source)
XLA Modules:
  0.0 111.3 jit_solution(6151113527227306310)
XLA Ops:
  0.6 108.8 %shard_map.122 = (bf16[1,64,2048]{2,1,0:T(8,128)(2,1)}, bf16[1,64,2048]{2,1,0:T(8,128)(2,1)}) custom-call(s32[8]{0:T(128)} %perm_ref.1, s32[8]{0:T(128)} %ablated_ref.1, bf16[1,64,2048]{2,1,0:T(8,128)(2,1)} %res_hbm.1, bf16[1,64,1024]{2,1,0:T(8,128)(2,1)} %q_hbm.1, bf16[1,64,512]{2,1,0:T(8,128)(2,1)} %k_hbm.1, bf16[1,64,512]{2,1,0:T(8,128)(2,1)} %v_hbm.1, ...), custom_call_target="tpu_custom_call" | custom-call | tf_op jit(solution)/shard_map/pallas_call | solution.py:558
  109.5 1.8 %shard_map.123 = (bf16[1,64,2048]{2,1,0:T(8,128)(2,1)}, bf16[1,64,2048]{2,1,0:T(8,128)(2,1)}) custom-call(bf16[1,64,2048]{2,1,0:T(8,128)(2,1)} %get-tuple-element.4.attn_ref, bf16[1,64,2048]{2,1,0:T(8,128)(2,1)} %get-tuple-element.5.mlp_ref), custom_call_target="tpu_custom_call" | custom-call | tf_op jit(solution)/shard_map/pallas_call | solution.py:614

commit v6 on v5

--- a/solution.py
+++ b/solution.py
@@ -55,7 +55,7 @@
     chunks = length // R
     _, _, owners, _, owned = line.shape
     pieces = w_buf.shape[0]
-    reuse = sum_r.shape[1]
+    reuse = hid_r.shape[1]
     units = chunks * pieces
     direct = min(DIRECT, units // (n - 1))
     half = chips * R
@@ -305,7 +305,7 @@
     way_of = (1, -1)
 
     def sum_copy(d, u, peer):
-        at = lax.rem(u, reuse)
+        at = lax.rem(u, sum_r.shape[1])
         return remote(own.at[d, u], got.at[d, u], sum_s.at[d], sum_r.at[d, at], mp=peer)
 
     def hid_copy(d, u, peer):
@@ -600,7 +600,7 @@
             dma((chunks,)),
             dma((chunks,)),
             dma((2,)),
-            dma((2, reuse)),
+            dma((2, min(units, LAG * (n - 1) + 2))),
             dma((4,)),
             dma((2, reuse)),
         ],
@@ -616,14 +616,14 @@
         in_specs=[anywhere, anywhere],
         out_specs=[anywhere, anywhere],
         out_shape=[out, out],
-        scratch_shapes=[pltpu.VMEM(out.shape, BF16), pltpu.VMEM(out.shape, BF16), dma((2, 2, 2))],
+        scratch_shapes=[pltpu.VMEM(out.shape, BF16), pltpu.VMEM(out.shape, BF16), dma((2, 2, 4))],
     )(attn, mlp)
 
 
 def place_kernel(attn_ref, mlp_ref, attn_out, mlp_out, attn_buf, mlp_buf, sem):
-    rows = attn_ref.shape[1] // 2
+    rows = attn_ref.shape[1] // 4
     pairs = ((attn_ref, attn_buf, attn_out), (mlp_ref, mlp_buf, mlp_out))
-    moves = [(i, j, pl.ds(j * rows, rows)) for j in range(2) for i in range(2)]
+    moves = [(i, j, pl.ds(j * rows, rows)) for j in range(4) for i in range(2)]
 
     def load(i, j, at):
         src, buf, dst = pairs[i]

time: 111 us -> 111 us (level)
  no operation moved by 1% of the time
where the time goes in v6:
time: 111 us
  Pallas kernels  110 us (99%)
    pallas_call x1, Pallas kernels, body(): pl.pallas_call(functools.partial(layer_kernel, nb, n, slots, w, joined),...  109 us

profile of v6, /device:TPU:0, one launch (start us, length us, event | category | flops | bytes accessed | tf_op | source)
XLA Modules:
  0.0 111.1 jit_solution(14512682551975220012)
XLA Ops:
  0.6 108.6 %shard_map.122 = (bf16[1,64,2048]{2,1,0:T(8,128)(2,1)}, bf16[1,64,2048]{2,1,0:T(8,128)(2,1)}) custom-call(s32[8]{0:T(128)} %perm_ref.1, s32[8]{0:T(128)} %ablated_ref.1, bf16[1,64,2048]{2,1,0:T(8,128)(2,1)} %res_hbm.1, bf16[1,64,1024]{2,1,0:T(8,128)(2,1)} %q_hbm.1, bf16[1,64,512]{2,1,0:T(8,128)(2,1)} %k_hbm.1, bf16[1,64,512]{2,1,0:T(8,128)(2,1)} %v_hbm.1, ...), custom_call_target="tpu_custom_call" | custom-call | tf_op jit(solution)/shard_map/pallas_call | solution.py:558
  109.3 1.8 %shard_map.123 = (bf16[1,64,2048]{2,1,0:T(8,128)(2,1)}, bf16[1,64,2048]{2,1,0:T(8,128)(2,1)}) custom-call(bf16[1,64,2048]{2,1,0:T(8,128)(2,1)} %get-tuple-element.4.attn_ref, bf16[1,64,2048]{2,1,0:T(8,128)(2,1)} %get-tuple-element.5.mlp_ref), custom_call_target="tpu_custom_call" | custom-call | tf_op jit(solution)/shard_map/pallas_call | solution.py:614
